TPU v7x, 256 devices: a whole 4x4x8 slice. The times are simulated.
256 devices in a mesh: rows: 8 (over z_lo, x), cols: 32 (over y, z_hi, core).
Axes of the slice: x: 4, y: 4, z: 8 (z_hi: 4, z_lo: 2; z = z_hi * 2 + z_lo), core: 2. Of those that a mesh axis runs over, the one named last changes fastest.
Arguments:
- image: bfloat16 [3, 512, 32768], P(None, 'rows', 'cols'), may hold values from -6 to 6
- w_patch: bfloat16 [48, 256], replicated, may hold values from -0.875 to 0.875
- dw_kernel: bfloat16 [7, 7, 256], replicated, may hold values from -0.875 to 0.875
- gain_one: float32 [256], replicated, may hold values from 0.25 to 1.75
- w_up: bfloat16 [256, 1024], replicated, may hold values from -0.375 to 0.375
- w_down: bfloat16 [1024, 256], replicated, may hold values from -0.1875 to 0.1875
- scale_block: float32 [256], replicated, may hold values from 0.25 to 1.75
- gain_two: float32 [256], replicated, may hold values from 0.25 to 1.75
- w_kv: bfloat16 [256, 2048], replicated, may hold values from -0.375 to 0.375
- latents: bfloat16 [128, 1024], replicated, may hold values from -0.75 to 0.75
- gain_three: float32 [1024], replicated, may hold values from 0.25 to 1.75
- w_q: bfloat16 [1024, 1024], replicated
- w_o: bfloat16 [1024, 1024], replicated, may hold values from -0.1875 to 0.1875
Outputs:
- encoded: float32 [128, 1024], replicated
All inputs are finite; a program needn't handle non-finite values.
Results may differ from a plain program's by a relative error of at most 0.0117.
The roundings to bfloat16 on the way count: a program that leaves them out, or rounds other values in their place, can miss the bound.
Values may be sent and summed in bfloat16 or wider, within the bound.
No kernel may reach another device: no remote copies, remote signals or barrier semaphores. Data moves between devices by JAX's collectives and lax.ppermute only.
A program may use at most 320 MiB of HBM per device.

v0:
```python
import jax
import jax.numpy as jnp
from jax import lax
from jax.sharding import PartitionSpec as P

HEADS = 8
HEAD_DIM = 128


def with_halo(value, sides, width):
    for axis, dim in sides:
        devices, length = (lax.axis_size(axis), value.shape[dim])
        up = [(i, (i + 1) % devices) for i in range(devices - 1)]
        down = [(j, i) for i, j in up]
        last = lax.slice_in_dim(value, length - width, length, axis=dim)
        initial = lax.slice_in_dim(value, 0, width, axis=dim)
        before = lax.ppermute(last, axis, up)
        after = lax.ppermute(initial, axis, down)
        value = jnp.concatenate([before, value, after], axis=dim)
    return value


def layer_norm(values, gain):
    center = values - jnp.mean(values, axis=-1, keepdims=True)
    spread = jnp.mean(center * center, axis=-1, keepdims=True)
    return center * lax.rsqrt(spread + 1e-06) * gain


def stem_patches(pixels, w_patch, grid_rows, grid_cols):
    patches = (
        pixels.reshape(3, grid_rows, 4, grid_cols, 4)
        .transpose(1, 3, 0, 2, 4)
        .reshape(grid_rows * grid_cols, 48)
    )
    embed = jnp.dot(patches, w_patch, preferred_element_type=jnp.float32).astype(jnp.bfloat16)
    return embed.reshape(grid_rows, grid_cols, w_patch.shape[1])


def body(
    image,
    w_patch,
    dw_kernel,
    gain_one,
    w_up,
    w_down,
    scale_block,
    gain_two,
    w_kv,
    latents,
    gain_three,
    w_q,
    w_o,
):
    tile_rows = image.shape[1] // 4
    tile_cols = image.shape[2] // 4
    count = tile_rows * tile_cols
    width = w_patch.shape[1]
    embed = stem_patches(image, w_patch, tile_rows, tile_cols)
    padded = with_halo(embed, (("rows", 0), ("cols", 1)), 3)
    kernel = dw_kernel.astype(jnp.float32)
    mixed = jnp.zeros((tile_rows, tile_cols, width), jnp.float32)
    for offset_row in range(7):
        for offset_col in range(7):
            mixed = (
                mixed
                + padded[
                    offset_row : offset_row + tile_rows, offset_col : offset_col + tile_cols
                ].astype(jnp.float32)
                * kernel[offset_row, offset_col]
            )
    normed = layer_norm(mixed.reshape(count, width), gain_one).astype(jnp.bfloat16)
    hidden = jax.nn.gelu(jnp.dot(normed, w_up, preferred_element_type=jnp.float32)).astype(
        jnp.bfloat16
    )
    block = embed.reshape(count, width).astype(jnp.float32) + scale_block * jnp.dot(
        hidden, w_down, preferred_element_type=jnp.float32
    )
    features = layer_norm(block, gain_two).astype(jnp.bfloat16)
    keyval = jnp.dot(features, w_kv, preferred_element_type=jnp.float32).astype(jnp.bfloat16)
    kv_width = HEADS * HEAD_DIM
    keys = keyval[:, :kv_width].reshape(count, HEADS, HEAD_DIM)
    values = keyval[:, kv_width:].reshape(count, HEADS, HEAD_DIM)
    lat_norm = layer_norm(latents.astype(jnp.float32), gain_three).astype(jnp.bfloat16)
    query = (
        jnp.dot(lat_norm, w_q, preferred_element_type=jnp.float32) * HEAD_DIM ** (-0.5)
    ).astype(jnp.bfloat16)
    query_heads = query.reshape(latents.shape[0], HEADS, HEAD_DIM)
    scores = jnp.einsum("lhd,thd->hlt", query_heads, keys, preferred_element_type=jnp.float32)
    top_local = jnp.max(scores, axis=-1)
    expo = jnp.exp(scores - top_local[:, :, None])
    total_local = jnp.sum(expo, axis=-1)
    accum_local = jnp.einsum(
        "hlt,thd->hld", expo.astype(jnp.bfloat16), values, preferred_element_type=jnp.float32
    )
    top_all = lax.pmax(top_local, ("rows", "cols"))
    factor = jnp.exp(top_local - top_all)
    total_all, accum_all = lax.psum(
        (total_local * factor, accum_local * factor[:, :, None]), ("rows", "cols")
    )
    attended = (
        (accum_all / total_all[:, :, None])
        .transpose(1, 0, 2)
        .reshape(latents.shape[0], kv_width)
        .astype(jnp.bfloat16)
    )
    return latents.astype(jnp.float32) + jnp.dot(attended, w_o, preferred_element_type=jnp.float32)


def solution(mesh):
    in_specs = (P(None, "rows", "cols"), P(), P(), P(), P(), P(), P(), P(), P(), P(), P(), P(), P())
    out_specs = P()
    return jax.shard_map(body, mesh=mesh, in_specs=in_specs, out_specs=out_specs, check_vma=False)
```

profile of v0, /device:TPU:1, one launch (start us, length us, event | category | flops | bytes accessed | tf_op | source)
XLA Modules:
  0.0 521.7 jit_solution(15387101142682252309)
XLA Ops:
  6.5 0.0 copy-start
  6.5 0.0 all-reduce.2.cloned.1.call-start
  6.5 28.9 %reshape.89 = bf16[3,16,4,256,4]{4,3,2,1,0:T(8,128)(2,1)} reshape(bf16[3,64,1024]{2,1,0:T(8,128)(2,1)} %param.13) | data formatting | bytes 786432 | tf_op jit(solution)/shard_map/reshape | solution.py:31
  35.4 10.5 %copy.18 = bf16[16,256,3,4,4]{1,0,4,3,2:T(8,128)(2,1)S(1)} copy(bf16[16,256,3,4,4]{4,1,3,0,2:T(8,128)(2,1)} %bitcast.95) | data formatting | bytes 786432 | tf_op jit(solution)/shard_map/transpose | solution.py:32
  45.9 0.0 copy-start.6
  45.9 0.0 copy-start.5
  46.0 0.0 copy-start.9
  46.0 0.1 copy.28
  46.1 0.7 convolution_convert_fusion.1
  46.9 0.1 fusion.59
  46.9 1.3 collective-permute-start.1
  48.2 4.6 collective-permute-start
  52.9 0.1 convert_reduce_fusion
  53.0 0.2 fusion.40
  53.3 0.0 copy-done
  53.3 0.0 copy-done.9
  53.3 0.5 fusion.37
  53.8 3.6 collective-permute-done.1
  57.4 0.9 collective-permute-done
  58.3 8.9 %collective-permute-start.2 = (bf16[22,3,256]{2,1,0:T(4,128)(2,1)S(1)}, bf16[22,3,256]{2,1,0:T(4,128)(2,1)S(1)}, u32[]{:S(2)}, u32[]{:S(2)}) collective-permute-start(bf16[22,3,256]{2,1,0:T(4,128)(2,1)S(1)} %get-tuple-element.13), channel_id=1, source_target_pairs={{0,1},{1,2},{2,3},{3,4},{4,5},{5,6},{6,7},{7,8},{8,9},{9,10},{10,1... | collective-permute-start | bytes 101384 | tf_op jit(solution)/shard_map/ppermute | solution.py:17
  67.2 2.1 collective-permute-start.3
  69.3 0.0 collective-permute-done.2
  69.3 4.1 collective-permute-done.3
  73.5 3.1 maximum_maximum_fusion
  76.6 37.4 %fusion.57 = (f32[16,256]{1,0:T(8,128)S(1)}, f32[16,256,256]{2,1,0:T(8,128)S(1)}) fusion(f32[256]{0:T(256)S(1)} %bitcast.156, bf16[22,259,256]{2,1,0:T(8,128)(2,1)S(1)} %get-tuple-element.12, f32[256]{0:T(256)S(1)} %bitcast.155, f32[256]{0:T(256)S(1)} %bitcast.154, f32[256]{0:T(256)S(1)} %bitcast.153, bf16[3,256,256]{2,1,0:T(8,128)(2,1)S(1)} %collective-permute-done.1, ...), kind=kLoop, calls=%fused_computation.83 | loop fusion | flops 160428032 | bytes 95224832 | tf_op jit(solution)/shard_map/reduce_sum | solution.py:24
  114.0 0.0 copy-start.10
  114.1 1.3 multiply_reduce_fusion.1
  115.4 0.0 copy-start.11
  115.4 0.0 copy-start.12
  115.5 0.0 copy-done.10
  115.5 3.3 fusion.25
  118.7 0.0 copy-done.12
  118.7 9.2 %fusion.63 = (f32[4096]{0:T(1024)S(1)}, f32[4096,256]{1,0:T(8,128)}) fusion(bf16[1024,256]{1,0:T(8,128)(2,1)S(1)} %copy-done.11, bf16[4096,256]{1,0:T(8,128)(2,1)} %fusion.25, bf16[256,1024]{1,0:T(8,128)(2,1)} %param.17, f32[256]{0:T(256)S(1)} %copy-done.12, bf16[4096,256]{1,0:T(8,128)(2,1)S(1)} %copy-done.3), kind=kOutput, calls=%fused_computation.89 | convolution fusion | flops 4336906240 | bytes 9454592 | tf_op jit(solution)/shard_map/dot_general | solution.py:75
  128.0 3.1 multiply_reduce_fusion
  131.1 0.3 copy-done.4
  131.4 9.5 %convolution_convert_fusion = bf16[4096,2048]{0,1:T(8,128)(2,1)} fusion(bf16[256,2048]{1,0:T(8,128)(2,1)} %param.21, f32[4096,256]{1,0:T(8,128)S(1)} %copy-done.4, f32[256]{0:T(256)S(1)} %copy-done.8, f32[4096]{0:T(1024)S(1)} %add_rsqrt_fusion, f32[4096]{0:T(1024)S(1)} %broadcast_multiply_fusion), kind=kOutput, calls=%fused_computation.10 | convolution fusion | flops 4307550208 | bytes 22053888 | tf_op jit(solution)/shard_map/dot_general | solution.py:79
  140.9 9.6 %fusion.58 = (bf16[4096,1024]{0,1:T(8,128)(2,1)S(1)}, bf16[4096,1024]{0,1:T(8,128)(2,1)}) fusion(bf16[4096,2048]{0,1:T(8,128)(2,1)} %convolution_convert_fusion), kind=kLoop, calls=%fused_computation.84 | loop fusion | bytes 33554432 | tf_op jit(solution)/shard_map/slice | solution.py:81
  150.5 8.1 %fusion.64 = (f32[8,128]{1,0:T(8,128)S(1)}, f32[8,128,4096]{2,1,0:T(8,128)}) fusion(bf16[4096,8,128]{0,2,1:T(8,128)(2,1)S(1)} %bitcast.96, bf16[16,8,8,128]{3,2,1,0:T(8,128)(2,1)S(1)} %fusion.37), kind=kOutput, calls=%fused_computation.90 | convolution fusion | flops 1077935104 | bytes 25432064 | tf_op jit(solution)/shard_map/lhd,thd->hlt/dot_general | solution.py:88
  158.5 83.7 %pmax.7 = f32[8,128]{1,0:T(8,128)S(1)} all-reduce(f32[8,128]{1,0:T(8,128)S(1)} %get-tuple-element.70), channel_id=1, replica_groups=mesh['rows'=8,'cols'=32] {'rows','cols'}, use_global_device_ids=true, to_apply=%region_7.0 | all-reduce | flops 1024 | bytes 8192 | tf_op jit(solution)/shard_map/pmax | solution.py:95
  242.2 8.1 %fusion.8 = f32[8,128]{1,0:T(8,128)S(1)} fusion(f32[8,128,4096]{2,1,0:T(8,128)} %get-tuple-element.71, f32[8,128]{1,0:T(8,128)S(1)} %get-tuple-element.70), kind=kLoop, calls=%fused_computation.11 | loop fusion | flops 8387584 | bytes 16785408 | tf_op jit(solution)/shard_map/reduce_sum | solution.py:91
  250.3 0.0 copy-start.1
  250.3 12.8 %fusion.33 = f32[8,128,128]{2,1,0:T(8,128)} fusion(bf16[4096,8,128]{0,2,1:T(8,128)(2,1)} %bitcast.100, f32[8,128,4096]{2,1,0:T(8,128)} %get-tuple-element.71, f32[8,128]{1,0:T(8,128)S(1)} %get-tuple-element.70, f32[8,128]{1,0:T(8,128)S(1)} %get-tuple-element.6), kind=kOutput, calls=%fused_computation.47 | convolution fusion | flops 1082261504 | bytes 25698304 | tf_op jit(solution)/shard_map/hlt,thd->hld/dot_general | solution.py:92
  263.2 0.0 all-reduce.2.cloned.1.call-update
  263.2 73.5 %psum.15 = f32[8,128]{1,0:T(8,128)S(1)} all-reduce(f32[8,128]{1,0:T(8,128)S(1)} %get-tuple-element.5), channel_id=1, replica_groups=mesh['rows'=8,'cols'=32] {'rows','cols'}, use_global_device_ids=true, to_apply=%region_10.0 | all-reduce | flops 1024 | bytes 8192 | tf_op jit(solution)/shard_map/psum | solution.py:97
  336.7 173.9 %all-reduce.2.cloned.1.call-done = f32[8,128,128]{2,1,0:T(8,128)} async-done(((f32[8,128,128]{2,1,0:T(8,128)}), f32[8,128,128]{2,1,0:T(8,128)}) %all-reduce.2.cloned.1.call-update) | async-done | bytes 524304 | tf_op jit(solution)/shard_map/psum | solution.py:97
  510.6 1.2 fusion.50
  511.8 0.2 copy.23
  512.0 2.9 convolution_add_fusion
  (26 shorter events, 0.2 us)
Async XLA Ops:
  6.5 46.7 %copy-start = (bf16[1024,1024]{1,0:T(8,128)(2,1)S(1)}, bf16[1024,1024]{1,0:T(8,128)(2,1)}, u32[]{:S(2)}) copy-start(bf16[1024,1024]{1,0:T(8,128)(2,1)} %param.24) | copy-start | bytes 6291460
  6.5 504.1 %all-reduce.2.cloned.1.call-start = ((), (), s32[]{:S(2)}) async-start(), calls=%async_computation | async-start | bytes 1048576 | tf_op jit(solution)/shard_map/psum | solution.py:97
  35.4 10.7 %copy-start.7 = (bf16[48,256]{1,0:T(8,128)(2,1)S(1)}, bf16[48,256]{1,0:T(8,128)(2,1)}, u32[]{:S(2)}) copy-start(bf16[48,256]{1,0:T(8,128)(2,1)} %param.14) | copy-start | bytes 73732
  45.9 6.9 %copy-start.6 = (bf16[7,7,256]{2,1,0:T(8,128)(2,1)S(1)}, bf16[7,7,256]{2,1,0:T(8,128)(2,1)}, u32[]{:S(2)}) copy-start(bf16[7,7,256]{2,1,0:T(8,128)(2,1)} %param.15) | copy-start | bytes 75268
  45.9 7.0 %copy-start.5 = (bf16[128,1024]{1,0:T(8,128)(2,1)S(1)}, bf16[128,1024]{1,0:T(8,128)(2,1)}, u32[]{:S(2)}) copy-start(bf16[128,1024]{1,0:T(8,128)(2,1)} %param.22) | copy-start | bytes 786436
  46.0 7.3 %copy-start.9 = (f32[1024]{0:T(1024)S(1)}, f32[1024]{0:T(1024)}, u32[]{:S(2)}) copy-start(f32[1024]{0:T(1024)} %param.23) | copy-start | bytes 12292
  46.9 29.7 %copy-start.2 = (bf16[4096,256]{1,0:T(8,128)(2,1)}, bf16[4096,256]{1,0:T(8,128)(2,1)S(1)}, u32[]{:S(2)}) copy-start(bf16[4096,256]{1,0:T(8,128)(2,1)S(1)} %convolution_convert_fusion.1) | copy-start | bytes 6291460
  46.9 10.4 %collective-permute-start.1 = (bf16[3,256,256]{2,1,0:T(8,128)(2,1)S(1)}, bf16[3,256,256]{2,1,0:T(8,128)(2,1)S(1)}, u32[]{:S(2)}, u32[]{:S(2)}) collective-permute-start(bf16[3,256,256]{2,1,0:T(8,128)(2,1)S(1)} %bitcast.105), channel_id=1, source_target_pairs={{32,0},{64,32},{96,64},{128,96},{160,128},{192,160},{224,192},{33,... | collective-permute-start | bytes 1179656 | tf_op jit(solution)/shard_map/ppermute | solution.py:18
  48.2 10.0 %collective-permute-start = (bf16[3,256,256]{2,1,0:T(8,128)(2,1)S(1)}, bf16[3,256,256]{2,1,0:T(8,128)(2,1)S(1)}, u32[]{:S(2)}, u32[]{:S(2)}) collective-permute-start(bf16[3,256,256]{2,1,0:T(8,128)(2,1)S(1)} %bitcast.104), channel_id=1, source_target_pairs={{0,32},{32,64},{64,96},{96,128},{128,160},{160,192},{192,224},{1,3... | collective-permute-start | bytes 1179656 | tf_op jit(solution)/shard_map/ppermute | solution.py:17
  58.3 11.0 %collective-permute-start.2 = (bf16[22,3,256]{2,1,0:T(4,128)(2,1)S(1)}, bf16[22,3,256]{2,1,0:T(4,128)(2,1)S(1)}, u32[]{:S(2)}, u32[]{:S(2)}) collective-permute-start(bf16[22,3,256]{2,1,0:T(4,128)(2,1)S(1)} %get-tuple-element.13), channel_id=1, source_target_pairs={{0,1},{1,2},{2,3},{3,4},{4,5},{5,6},{6,7},{7,8},{8,9},{9,10},{10,1... | collective-permute-start | bytes 101384 | tf_op jit(solution)/shard_map/ppermute | solution.py:17
  67.2 6.3 %collective-permute-start.3 = (bf16[22,3,256]{2,1,0:T(4,128)(2,1)S(1)}, bf16[22,3,256]{2,1,0:T(4,128)(2,1)S(1)}, u32[]{:S(2)}, u32[]{:S(2)}) collective-permute-start(bf16[22,3,256]{2,1,0:T(4,128)(2,1)S(1)} %get-tuple-element.14), channel_id=1, source_target_pairs={{1,0},{2,1},{3,2},{4,3},{5,4},{6,5},{7,6},{8,7},{9,8},{10,9},{11,1... | collective-permute-start | bytes 101384 | tf_op jit(solution)/shard_map/ppermute | solution.py:18
  114.0 1.4 copy-start.10
  115.4 3.3 copy-start.3
  115.4 3.3 copy-start.11
  115.4 3.3 copy-start.12
  127.9 3.4 copy-start.4
  127.9 3.4 copy-start.8
  250.3 264.6 %copy-start.1 = (bf16[1024,1024]{1,0:T(8,128)(2,1)S(1)}, bf16[1024,1024]{1,0:T(8,128)(2,1)}, u32[]{:S(2)}) copy-start(bf16[1024,1024]{1,0:T(8,128)(2,1)} %param.24) | copy-start | bytes 6291460
Sparse Core Ops, SparseCore 0:
  263.3 247.2 all-reduce.1
where the time goes:
time: 523 us; the launch traced here: 522 us
  waiting for transfers between devices  183 us (35%)
  blocking collectives  157 us (30%)
  other arithmetic  58 us (11%)
  local copies, waits for them, and re-layouts  49.7 us (10%)
  matrix products  43.7 us (8%)
  starting transfers between devices  16.9 us (3%)
  between operations  13.7 us (3%)
    psum x1, waiting for transfers between devices, body(): lax.psum((total_local * factor, accum_local * factor[:, :, None]), ('rows...  174 us
    pmax x1, blocking collectives, body(): top_all = lax.pmax(top_local, ('rows', 'cols'))  83.7 us
    psum x1, blocking collectives, body(): lax.psum((total_local * factor, accum_local * factor[:, :, None]), ('rows...  73.5 us
    reduce_sum x2, other arithmetic, layer_norm(): center = values - jnp.mean(values, axis=-1, keepdims=True)  37.5 us
    reshape x1, local copies, waits for them, and re-layouts, stem_patches(): pixels.reshape(3, grid_rows, 4, grid_cols, 4).transpose(1, 3, 0, 2, 4)  28.9 us
    ppermute x2, starting transfers between devices, with_halo(): before = lax.ppermute(last, axis, up)  13.5 us
    dot_general x1, matrix products, body(): jnp.einsum('hlt,thd->hld', expo.astype(jnp.bfloat16), values, preferred_e...  12.8 us
    transpose x1, local copies, waits for them, and re-layouts, stem_patches(): patches = pixels.reshape(3, grid_rows, 4, grid_cols, 4).transpose(1, 3, 0...  10.5 us
  transfers between devices with their start and end apart: 5, of which 4 were waited for; matrix products, arithmetic and copies ran while one was open for 0% of the time, Pallas kernels for 0%

commit v1 on v0

--- a/solution.py
+++ b/solution.py
@@ -34,6 +34,36 @@
     )
     embed = jnp.dot(patches, w_patch, preferred_element_type=jnp.float32).astype(jnp.bfloat16)
     return embed.reshape(grid_rows, grid_cols, w_patch.shape[1])
+
+
+def split_three(value):
+    high = lax.reduce_precision(value, 8, 7)
+    rest = value - high
+    middle = lax.reduce_precision(rest, 8, 7)
+    return high, middle, rest - middle
+
+
+def pack_partial(sums, top, total):
+    rows = jnp.stack([*split_three(top), *split_three(total)], axis=-2)
+    rows = jnp.pad(rows, ((0, 0),) * (rows.ndim - 2) + ((0, 10), (0, 0)))
+    return jnp.concatenate([sums, rows], axis=-2).astype(jnp.bfloat16)
+
+
+def merge_partials(packed):
+    packed = packed.astype(jnp.float32)
+    count = packed.shape[1] - 16
+    stats = packed[:, count:]
+    top = (stats[:, 0] + stats[:, 1]) + stats[:, 2]
+    total = (stats[:, 3] + stats[:, 4]) + stats[:, 5]
+    top_all = jnp.max(top, axis=0)
+    factor = jnp.exp(top - top_all)
+    sums = jnp.sum(packed[:, :count] * factor[:, None], axis=0)
+    return sums, top_all, jnp.sum(total * factor, axis=0)
+
+
+def share(value, axis):
+    size = lax.axis_size(axis)
+    return lax.all_to_all(jnp.broadcast_to(value, (size, *value.shape)), axis, 0, 0)
 
 
 def body(
@@ -92,18 +122,18 @@
     accum_local = jnp.einsum(
         "hlt,thd->hld", expo.astype(jnp.bfloat16), values, preferred_element_type=jnp.float32
     )
-    top_all = lax.pmax(top_local, ("rows", "cols"))
-    factor = jnp.exp(top_local - top_all)
-    total_all, accum_all = lax.psum(
-        (total_local * factor, accum_local * factor[:, :, None]), ("rows", "cols")
+    cols = lax.axis_size("cols")
+    per_head = cols // HEADS
+    sums = accum_local.transpose(0, 2, 1).reshape(cols, kv_width // cols, -1)
+    packed = pack_partial(
+        sums, jnp.repeat(top_local, per_head, axis=0), jnp.repeat(total_local, per_head, axis=0)
     )
-    attended = (
-        (accum_all / total_all[:, :, None])
-        .transpose(1, 0, 2)
-        .reshape(latents.shape[0], kv_width)
-        .astype(jnp.bfloat16)
+    partial = merge_partials(lax.all_to_all(packed, "cols", 0, 0))
+    sums, _, total = merge_partials(share(pack_partial(*partial), "rows"))
+    attended = share((sums / total).astype(jnp.bfloat16), "cols").reshape(kv_width, -1)
+    return latents.astype(jnp.float32) + lax.dot_general(
+        attended, w_o, (((0,), (0,)), ((), ())), preferred_element_type=jnp.float32
     )
-    return latents.astype(jnp.float32) + jnp.dot(attended, w_o, preferred_element_type=jnp.float32)
 
 
 def solution(mesh):

time: 523 us -> 231 us (0.44)
  waiting for transfers between devices: 183 us -> 8.61 us
  blocking collectives: 157 us -> 55.3 us
  between operations: 13.7 us -> 0.45 us
    psum x1 -> x0, waiting for transfers between devices: 174 us -> none  [body(): lax.psum((total_local * factor, accum_local * factor[:, :, None]), ('rows...]
    pmax x1 -> x0, blocking collectives: 83.7 us -> none  [body(): top_all = lax.pmax(top_local, ('rows', 'cols'))]
    psum x1 -> x0, blocking collectives: 73.5 us -> none  [body(): lax.psum((total_local * factor, accum_local * factor[:, :, None]), ('rows...]
    all_to_all x0 -> x3, blocking collectives: none -> 55.3 us  [the longest x2 30.4 us: share(): lax.all_to_all(jnp.broadcast_to(value, (size, *value.shape)), axis, 0, 0)]
  transfers between devices with their start and end apart: 5 -> 4, of which waited for: 4 -> 3; matrix products, arithmetic and copies ran while one was open for 0% -> 0% of each run, Pallas kernels for 0% -> 0%
where the time goes in v1:
time: 231 us; the launch traced here: 230 us
  other arithmetic  57.2 us (25%)
  blocking collectives  55.3 us (24%)
  local copies, waits for them, and re-layouts  49.7 us (22%)
  matrix products  41.8 us (18%)
  starting transfers between devices  16.9 us (7%)
  waiting for transfers between devices  8.61 us (4%)
    reduce_sum x2, other arithmetic, layer_norm(): center = values - jnp.mean(values, axis=-1, keepdims=True)  37.5 us
    all_to_all x2, blocking collectives, share(): lax.all_to_all(jnp.broadcast_to(value, (size, *value.shape)), axis, 0, 0)  30.4 us
    reshape x1, local copies, waits for them, and re-layouts, stem_patches(): pixels.reshape(3, grid_rows, 4, grid_cols, 4).transpose(1, 3, 0, 2, 4)  28.9 us
    all_to_all x1, blocking collectives, body(): partial = merge_partials(lax.all_to_all(packed, 'cols', 0, 0))  24.9 us
    ppermute x2, starting transfers between devices, with_halo(): before = lax.ppermute(last, axis, up)  13.5 us
    dot_general x1, matrix products, body(): jnp.einsum('hlt,thd->hld', expo.astype(jnp.bfloat16), values, preferred_e...  11 us
    transpose x1, local copies, waits for them, and re-layouts, stem_patches(): patches = pixels.reshape(3, grid_rows, 4, grid_cols, 4).transpose(1, 3, 0...  10.5 us
    slice x1, local copies, waits for them, and re-layouts, body(): values = keyval[:, kv_width:].reshape(count, HEADS, HEAD_DIM)  9.53 us
  transfers between devices with their start and end apart: 4, of which 3 were waited for; matrix products, arithmetic and copies ran while one was open for 0% of the time, Pallas kernels for 0%

profile of v1, /device:TPU:1, one launch (start us, length us, event | category | flops | bytes accessed | tf_op | source)
XLA Modules:
  0.0 230.0 jit_solution(6284285061255844264)
XLA Ops:
  0.0 0.0 copy-start
  0.0 28.9 %reshape.238 = bf16[3,16,4,256,4]{4,3,2,1,0:T(8,128)(2,1)} reshape(bf16[3,64,1024]{2,1,0:T(8,128)(2,1)} %param.13) | data formatting | bytes 786432 | tf_op jit(solution)/shard_map/reshape | solution.py:31
  28.9 10.5 %copy.51 = bf16[16,256,3,4,4]{1,0,4,3,2:T(8,128)(2,1)S(1)} copy(bf16[16,256,3,4,4]{4,1,3,0,2:T(8,128)(2,1)} %bitcast.138) | data formatting | bytes 786432 | tf_op jit(solution)/shard_map/transpose | solution.py:32
  39.4 0.0 copy-start.6
  39.4 0.0 copy-start.5
  39.4 0.0 copy-start.9
  39.4 0.1 copy.72
  39.6 0.0 copy-done.7
  39.6 0.7 convolution_convert_fusion.1
  40.3 0.0 copy-start.2
  40.3 0.1 fusion.75
  40.4 1.3 collective-permute-start.1
  41.7 4.6 %collective-permute-start = (bf16[3,256,256]{2,1,0:T(8,128)(2,1)S(1)}, bf16[3,256,256]{2,1,0:T(8,128)(2,1)S(1)}, u32[]{:S(2)}, u32[]{:S(2)}) collective-permute-start(bf16[3,256,256]{2,1,0:T(8,128)(2,1)S(1)} %bitcast.148), channel_id=1, source_target_pairs={{0,32},{32,64},{64,96},{96,128},{128,160},{160,192},{192,224},{1,3... | collective-permute-start | bytes 1179656 | tf_op jit(solution)/shard_map/ppermute | solution.py:17
  46.3 0.0 copy-done.6
  46.4 0.0 copy-done.5
  46.4 0.1 convert_reduce_fusion
  46.5 0.2 fusion.41
  46.7 0.0 copy-done
  46.8 0.5 fusion.37
  47.2 3.6 %collective-permute-done.1 = bf16[3,256,256]{2,1,0:T(8,128)(2,1)S(1)} collective-permute-done((bf16[3,256,256]{2,1,0:T(8,128)(2,1)S(1)}, bf16[3,256,256]{2,1,0:T(8,128)(2,1)S(1)}, u32[]{:S(2)}, u32[]{:S(2)}) %collective-permute-start.1) | collective-permute-done | bytes 393248 | tf_op jit(solution)/shard_map/ppermute | solution.py:18
  50.8 0.9 collective-permute-done
  51.8 8.9 %collective-permute-start.2 = (bf16[22,3,256]{2,1,0:T(4,128)(2,1)S(1)}, bf16[22,3,256]{2,1,0:T(4,128)(2,1)S(1)}, u32[]{:S(2)}, u32[]{:S(2)}) collective-permute-start(bf16[22,3,256]{2,1,0:T(4,128)(2,1)S(1)} %get-tuple-element.15), channel_id=1, source_target_pairs={{0,1},{1,2},{2,3},{3,4},{4,5},{5,6},{6,7},{7,8},{8,9},{9,10},{10,1... | collective-permute-start | bytes 101384 | tf_op jit(solution)/shard_map/ppermute | solution.py:17
  60.7 2.1 collective-permute-start.3
  62.8 0.0 collective-permute-done.2
  62.8 4.1 %collective-permute-done.3 = bf16[22,3,256]{2,1,0:T(4,128)(2,1)S(1)} collective-permute-done((bf16[22,3,256]{2,1,0:T(4,128)(2,1)S(1)}, bf16[22,3,256]{2,1,0:T(4,128)(2,1)S(1)}, u32[]{:S(2)}, u32[]{:S(2)}) %collective-permute-start.3) | collective-permute-done | bytes 33824 | tf_op jit(solution)/shard_map/ppermute | solution.py:18
  66.9 3.1 %maximum_maximum_fusion = (bf16[22,259,256]{2,1,0:T(8,128)(2,1)S(1)}, bf16[22,259,256]{2,1,0:T(8,128)(2,1)S(1)}) fusion(bf16[3,256,256]{2,1,0:T(8,128)(2,1)S(1)} %collective-permute-done.1, bf16[16,256,256]{2,1,0:T(8,128)(2,1)S(1)} %bitcast.141, bf16[3,256,256]{2,1,0:T(8,128)(2,1)S(1)} %collective-permute-done, ...), kind=kLoop, calls=%fused_computation.32 | loop fusion | flops 23339008 | bytes 8785920 | tf_op jit(solution)/shard_map/concatenate | solution.py:19
  70.1 37.4 %fusion.73 = (f32[16,256]{1,0:T(8,128)S(1)}, f32[16,256,256]{2,1,0:T(8,128)S(1)}) fusion(f32[256]{0:T(256)S(1)} %bitcast.214, bf16[22,259,256]{2,1,0:T(8,128)(2,1)S(1)} %get-tuple-element.14, f32[256]{0:T(256)S(1)} %bitcast.213, f32[256]{0:T(256)S(1)} %bitcast.212, f32[256]{0:T(256)S(1)} %bitcast.211, bf16[3,256,256]{2,1,0:T(8,128)(2,1)S(1)} %collective-permute-done.1, ...), kind=kLoop, calls=%fused_computation.134 | loop fusion | flops 160428032 | bytes 95224832 | tf_op jit(solution)/shard_map/reduce_sum | solution.py:24
  107.5 0.0 copy-start.10
  107.5 1.3 multiply_reduce_fusion.1
  108.9 0.0 copy-start.11
  108.9 0.0 copy-start.12
  108.9 3.3 %fusion.25 = bf16[4096,256]{1,0:T(8,128)(2,1)} fusion(f32[16,256,256]{2,1,0:T(8,128)S(1)} %get-tuple-element.10, f32[256]{0:T(256)S(1)} %copy-done.10, f32[4096]{0:T(1024)S(1)} %bitcast.157, f32[4096]{0:T(1024)S(1)} %bitcast.156), kind=kLoop, calls=%fused_computation.23 | loop fusion | flops 4194304 | bytes 6325248 | tf_op jit(solution)/shard_map/convert_element_type | solution.py:101
  112.2 0.0 copy-done.11
  112.2 9.2 %fusion.81 = (f32[4096]{0:T(1024)S(1)}, f32[4096,256]{1,0:T(8,128)}) fusion(bf16[1024,256]{1,0:T(8,128)(2,1)S(1)} %copy-done.11, bf16[4096,256]{1,0:T(8,128)(2,1)} %fusion.25, bf16[256,1024]{1,0:T(8,128)(2,1)} %param.17, f32[256]{0:T(256)S(1)} %copy-done.12, bf16[4096,256]{1,0:T(8,128)(2,1)S(1)} %copy-done.3), kind=kOutput, calls=%fused_computation.142 | convolution fusion | flops 4336906240 | bytes 9454592 | tf_op jit(solution)/shard_map/dot_general | solution.py:105
  121.4 3.1 %multiply_reduce_fusion = f32[4096]{0:T(1024)S(1)} fusion(f32[4096,256]{1,0:T(8,128)} %get-tuple-element.83, f32[4096]{0:T(1024)S(1)} %broadcast_multiply_fusion), kind=kLoop, calls=%fused_computation.25 | loop fusion | flops 3141632 | bytes 4227072 | tf_op jit(solution)/shard_map/reduce_sum | solution.py:25
  124.6 0.3 copy-done.4
  124.9 9.5 %convolution_convert_fusion = bf16[4096,2048]{0,1:T(8,128)(2,1)} fusion(bf16[256,2048]{1,0:T(8,128)(2,1)} %param.21, f32[4096,256]{1,0:T(8,128)S(1)} %copy-done.4, f32[256]{0:T(256)S(1)} %copy-done.8, f32[4096]{0:T(1024)S(1)} %add_rsqrt_fusion, f32[4096]{0:T(1024)S(1)} %broadcast_multiply_fusion), kind=kOutput, calls=%fused_computation.10 | convolution fusion | flops 4307550208 | bytes 22053888 | tf_op jit(solution)/shard_map/dot_general | solution.py:109
  134.4 9.5 %fusion.74 = (bf16[4096,1024]{0,1:T(8,128)(2,1)}, bf16[4096,1024]{0,1:T(8,128)(2,1)S(1)}) fusion(bf16[4096,2048]{0,1:T(8,128)(2,1)} %convolution_convert_fusion), kind=kLoop, calls=%fused_computation.135 | loop fusion | bytes 33554432 | tf_op jit(solution)/shard_map/slice | solution.py:112
  143.9 8.1 %fusion.82 = (f32[8,128]{1,0:T(8,128)S(1)}, f32[8,128,4096]{2,1,0:T(8,128)}) fusion(bf16[4096,8,128]{0,2,1:T(8,128)(2,1)S(1)} %bitcast.139, bf16[16,8,8,128]{3,2,1,0:T(8,128)(2,1)S(1)} %fusion.37), kind=kOutput, calls=%fused_computation.143 | convolution fusion | flops 1077935104 | bytes 25432064 | tf_op jit(solution)/shard_map/lhd,thd->hlt/dot_general | solution.py:118
  152.0 8.1 %fusion.8 = f32[8,128]{1,0:T(8,128)S(1)} fusion(f32[8,128,4096]{2,1,0:T(8,128)} %get-tuple-element.85, f32[8,128]{1,0:T(8,128)S(1)} %get-tuple-element.84), kind=kLoop, calls=%fused_computation.11 | loop fusion | flops 8387584 | bytes 16785408 | tf_op jit(solution)/shard_map/reduce_sum | solution.py:121
  160.1 11.0 %fusion.34 = bf16[8,128,128]{2,1,0:T(8,128)(2,1)S(1)} fusion(bf16[4096,8,128]{0,2,1:T(8,128)(2,1)} %bitcast.143, f32[8,128,4096]{2,1,0:T(8,128)} %get-tuple-element.85, f32[8,128]{1,0:T(8,128)S(1)} %get-tuple-element.84), kind=kOutput, calls=%fused_computation.50 | convolution fusion | flops 1082261504 | bytes 25432064 | tf_op jit(solution)/shard_map/hlt,thd->hld/dot_general | solution.py:122
  171.2 0.0 copy-start.1
  171.2 24.9 %all_to_all.15 = bf16[32,48,128]{2,1,0:T(8,128)(2,1)S(1)} all-to-all(bf16[32,48,128]{2,1,0:T(8,128)(2,1)S(1)} %fusion.45), channel_id=1, replica_groups=mesh['rows'=8,'cols'=32] {'cols'}, dimensions={0} | all-to-all | bytes 786432 | tf_op jit(solution)/shard_map/all_to_all | solution.py:131
  196.1 0.1 convert_element_type.256
  196.3 0.1 fusion.44
  196.5 12.5 %all_to_all.16 = bf16[8,48,128]{2,1,0:T(8,128)(2,1)S(1)} all-to-all(bf16[8,48,128]{2,1,0:T(8,128)(2,1)S(1)} %broadcast_in_dim.10), channel_id=1, replica_groups=mesh['rows'=8,'cols'=32] {'rows'}, dimensions={0} | all-to-all | bytes 196608 | tf_op jit(solution)/shard_map/all_to_all | solution.py:66
  209.2 18.0 %all_to_all.17 = bf16[32,32,128]{2,1,0:T(8,128)(2,1)S(1)} all-to-all(bf16[32,32,128]{2,1,0:T(8,128)(2,1)S(1)} %broadcast_in_dim.11), channel_id=1, replica_groups=mesh['rows'=8,'cols'=32] {'cols'}, dimensions={0} | all-to-all | bytes 524288 | tf_op jit(solution)/shard_map/all_to_all | solution.py:66
  227.1 2.9 %convolution_add_fusion = f32[128,1024]{1,0:T(8,128)} fusion(bf16[1024,128]{1,0:T(8,128)(2,1)S(1)} %bitcast.147, bf16[1024,1024]{1,0:T(8,128)(2,1)} %param.25, bf16[128,1024]{1,0:T(8,128)(2,1)S(1)} %copy-done.5), kind=kOutput, calls=%fused_computation.47 | convolution fusion | flops 268697600 | bytes 3145728 | tf_op jit(solution)/shard_map/dot_general | solution.py:134
  (51 shorter events, 0.7 us)
Async XLA Ops:
  0.0 46.7 %copy-start = (bf16[1024,1024]{1,0:T(8,128)(2,1)S(1)}, bf16[1024,1024]{1,0:T(8,128)(2,1)}, u32[]{:S(2)}) copy-start(bf16[1024,1024]{1,0:T(8,128)(2,1)} %param.24) | copy-start | bytes 6291460
  28.9 10.7 %copy-start.7 = (bf16[48,256]{1,0:T(8,128)(2,1)S(1)}, bf16[48,256]{1,0:T(8,128)(2,1)}, u32[]{:S(2)}) copy-start(bf16[48,256]{1,0:T(8,128)(2,1)} %param.14) | copy-start | bytes 73732
  39.4 6.9 %copy-start.6 = (bf16[7,7,256]{2,1,0:T(8,128)(2,1)S(1)}, bf16[7,7,256]{2,1,0:T(8,128)(2,1)}, u32[]{:S(2)}) copy-start(bf16[7,7,256]{2,1,0:T(8,128)(2,1)} %param.15) | copy-start | bytes 75268
  39.4 7.0 %copy-start.5 = (bf16[128,1024]{1,0:T(8,128)(2,1)S(1)}, bf16[128,1024]{1,0:T(8,128)(2,1)}, u32[]{:S(2)}) copy-start(bf16[128,1024]{1,0:T(8,128)(2,1)} %param.22) | copy-start | bytes 786436
  39.4 7.3 %copy-start.9 = (f32[1024]{0:T(1024)S(1)}, f32[1024]{0:T(1024)}, u32[]{:S(2)}) copy-start(f32[1024]{0:T(1024)} %param.23) | copy-start | bytes 12292
  40.3 29.7 %copy-start.2 = (bf16[4096,256]{1,0:T(8,128)(2,1)}, bf16[4096,256]{1,0:T(8,128)(2,1)S(1)}, u32[]{:S(2)}) copy-start(bf16[4096,256]{1,0:T(8,128)(2,1)S(1)} %convolution_convert_fusion.1) | copy-start | bytes 6291460
  40.4 10.4 %collective-permute-start.1 = (bf16[3,256,256]{2,1,0:T(8,128)(2,1)S(1)}, bf16[3,256,256]{2,1,0:T(8,128)(2,1)S(1)}, u32[]{:S(2)}, u32[]{:S(2)}) collective-permute-start(bf16[3,256,256]{2,1,0:T(8,128)(2,1)S(1)} %bitcast.149), channel_id=1, source_target_pairs={{32,0},{64,32},{96,64},{128,96},{160,128},{192,160},{224,192},{33,... | collective-permute-start | bytes 1179656 | tf_op jit(solution)/shard_map/ppermute | solution.py:18
  41.7 10.0 %collective-permute-start = (bf16[3,256,256]{2,1,0:T(8,128)(2,1)S(1)}, bf16[3,256,256]{2,1,0:T(8,128)(2,1)S(1)}, u32[]{:S(2)}, u32[]{:S(2)}) collective-permute-start(bf16[3,256,256]{2,1,0:T(8,128)(2,1)S(1)} %bitcast.148), channel_id=1, source_target_pairs={{0,32},{32,64},{64,96},{96,128},{128,160},{160,192},{192,224},{1,3... | collective-permute-start | bytes 1179656 | tf_op jit(solution)/shard_map/ppermute | solution.py:17
  51.8 11.0 %collective-permute-start.2 = (bf16[22,3,256]{2,1,0:T(4,128)(2,1)S(1)}, bf16[22,3,256]{2,1,0:T(4,128)(2,1)S(1)}, u32[]{:S(2)}, u32[]{:S(2)}) collective-permute-start(bf16[22,3,256]{2,1,0:T(4,128)(2,1)S(1)} %get-tuple-element.15), channel_id=1, source_target_pairs={{0,1},{1,2},{2,3},{3,4},{4,5},{5,6},{6,7},{7,8},{8,9},{9,10},{10,1... | collective-permute-start | bytes 101384 | tf_op jit(solution)/shard_map/ppermute | solution.py:17
  60.7 6.3 %collective-permute-start.3 = (bf16[22,3,256]{2,1,0:T(4,128)(2,1)S(1)}, bf16[22,3,256]{2,1,0:T(4,128)(2,1)S(1)}, u32[]{:S(2)}, u32[]{:S(2)}) collective-permute-start(bf16[22,3,256]{2,1,0:T(4,128)(2,1)S(1)} %get-tuple-element.16), channel_id=1, source_target_pairs={{1,0},{2,1},{3,2},{4,3},{5,4},{6,5},{7,6},{8,7},{9,8},{10,9},{11,1... | collective-permute-start | bytes 101384 | tf_op jit(solution)/shard_map/ppermute | solution.py:18
  107.5 1.4 copy-start.10
  108.9 3.3 %copy-start.3 = (bf16[4096,256]{1,0:T(8,128)(2,1)S(1)}, bf16[4096,256]{1,0:T(8,128)(2,1)}, u32[]{:S(2)}) copy-start(bf16[4096,256]{1,0:T(8,128)(2,1)} %copy-done.2) | copy-start | bytes 6291460
  108.9 3.3 %copy-start.11 = (bf16[1024,256]{1,0:T(8,128)(2,1)S(1)}, bf16[1024,256]{1,0:T(8,128)(2,1)}, u32[]{:S(2)}) copy-start(bf16[1024,256]{1,0:T(8,128)(2,1)} %param.18) | copy-start | bytes 1572868
  108.9 3.3 %copy-start.12 = (f32[256]{0:T(256)S(1)}, f32[256]{0:T(256)}, u32[]{:S(2)}) copy-start(f32[256]{0:T(256)} %param.19) | copy-start | bytes 3076
  121.4 3.4 %copy-start.4 = (f32[4096,256]{1,0:T(8,128)S(1)}, f32[4096,256]{1,0:T(8,128)}, u32[]{:S(2)}) copy-start(f32[4096,256]{1,0:T(8,128)} %get-tuple-element.83) | copy-start | bytes 12582916
  121.4 3.4 %copy-start.8 = (f32[256]{0:T(256)S(1)}, f32[256]{0:T(256)}, u32[]{:S(2)}) copy-start(f32[256]{0:T(256)} %param.20) | copy-start | bytes 3076
  171.2 58.8 %copy-start.1 = (bf16[1024,1024]{1,0:T(8,128)(2,1)S(1)}, bf16[1024,1024]{1,0:T(8,128)(2,1)}, u32[]{:S(2)}) copy-start(bf16[1024,1024]{1,0:T(8,128)(2,1)} %param.24) | copy-start | bytes 6291460

commit v2 on v1

v2 whole, which is shorter than its diff:
```python
import jax
import jax.numpy as jnp
from jax import lax
from jax.experimental import pallas as pl
from jax.experimental.pallas import tpu as pltpu
from jax.sharding import PartitionSpec as P

HEADS = 8
HEAD_DIM = 128
F32 = jnp.float32
BF16 = jnp.bfloat16
TOKENS = 512


def exchange(value, axis, dim, width):
    devices, length = lax.axis_size(axis), value.shape[dim]
    up = [(i, i + 1) for i in range(devices - 1)]
    down = [(j, i) for i, j in up]
    before = lax.ppermute(lax.slice_in_dim(value, length - width, length, axis=dim), axis, up)
    after = lax.ppermute(lax.slice_in_dim(value, 0, width, axis=dim), axis, down)
    return before, after


def layer_norm(values, gain):
    center = values - jnp.mean(values, axis=-1, keepdims=True)
    spread = jnp.mean(center * center, axis=-1, keepdims=True)
    return center * lax.rsqrt(spread + 1e-06) * gain


def matmul(left, right, dims=((1,), (0,))):
    return lax.dot_general(left, right, (dims, ((), ())), preferred_element_type=F32)


def iota(shape, dim):
    return lax.broadcasted_iota(jnp.int32, shape, dim)


def ones_where(mask):
    return jnp.where(mask, 1.0, 0.0).astype(BF16)


def stem(image, side, edge, w_patch, embed, ordered, pixels):
    rows = embed.shape[0]
    local = (rows - 6) * 4
    places = rows * 16
    place, source = iota((places, 3 * local), 0), iota((places, 3 * local), 1)
    slot = place % 16
    pixel_row = (place // 16) * 4 + slot % 4
    channel = slot // 4
    inside = (slot < 12) & (pixel_row >= 12) & (pixel_row < 12 + local)
    pick = ones_where(inside & (source == channel * local + pixel_row - 12))
    place, source = iota((places, 96), 0), iota((places, 96), 1)
    slot = place % 16
    pixel_row = (place // 16) * 4 + slot % 4
    channel = slot // 4
    upper = (pixel_row < 12) & (source == channel * 16 + pixel_row)
    lower = (pixel_row >= 12 + local) & (source == 48 + channel * 16 + pixel_row - 12 - local)
    pick_edge = ones_where((slot < 12) & (upper | lower))
    width = image.shape[1]
    for start in range(0, width, 256):
        lanes = slice(start, start + 256)
        ordered[:, lanes] = (
            matmul(pick, image[:, lanes]) + matmul(pick_edge, edge[:, lanes])
        ).astype(BF16)
    ordered[:, width:] = (
        matmul(pick, side[...]) + matmul(pick_edge, edge[:, width:])
    ).astype(BF16)
    lane, pixel = iota((512, 512), 1), iota((512, 512), 0)
    split = ones_where(pixel == 4 * (lane % 128) + lane // 128)
    for part in range(width // 512):
        found = matmul(ordered[:, part * 512 : part * 512 + 512], split).astype(BF16)
        for phase in range(4):
            pixels[phase, :, part * 128 : part * 128 + 128] = found[:, phase * 128 : phase * 128 + 128]
    lane, pixel = iota((128, 512), 1), iota((128, 512), 0)
    split = ones_where((pixel < 24) & (pixel == 4 * (lane % 128 - 5) + lane // 128))
    found = matmul(ordered[:, width:], split).astype(BF16)
    columns = width // 4
    for phase in range(4):
        pixels[phase, :, columns:] = found[:, phase * 128 : phase * 128 + 128]
    place, source = iota((64, 48), 0), iota((64, 48), 1)
    slot = place % 16
    pick = ones_where((slot < 12) & (source == slot * 4 + place // 16))
    weights = matmul(pick, w_patch[...]).astype(BF16)

    def step(row, carry):
        patches = jnp.concatenate(
            [pixels[phase, pl.ds(pl.multiple_of(row * 16, 16), 16), :] for phase in range(4)], axis=0
        )
        value = matmul(patches, weights, ((0,), (0,))).astype(BF16).astype(F32)
        blocks = columns // 8
        embed[row, 1 : blocks + 1] = value[:columns].reshape(blocks, 8, -1)
        embed[row, 0] = value[columns : columns + 8]
        embed[row, blocks + 1] = value[columns + 8 : columns + 16]
        return carry

    lax.fori_loop(0, rows, step, 0)


def conv_tile(embed, taps, mixed_ref, row, store_row, rows=2, blocks=8):
    columns = embed.shape[1] - 2
    row_in_lane = iota((1, 8, 128), 1)
    chunks = columns // blocks

    def step(index, carry):
        block = (index % chunks) * blocks
        half = index // chunks
        lanes = pl.ds(pl.multiple_of(half * 128, 128), 128)
        mixed = [None] * rows
        for shift in range(7):
            first, rest = divmod(5 + shift, 8)
            count = blocks + (1 if rest else 0)
            sums = [None] * rows
            weights = [taps[i * 7 + shift, :, lanes] for i in range(7)]
            for line in range(rows + 6):
                value = embed[row + line, pl.ds(block + first, count), :, lanes]
                for r in range(rows):
                    if 0 <= line - r < 7:
                        term = value * weights[line - r]
                        sums[r] = term if sums[r] is None else sums[r] + term
            for r in range(rows):
                total = sums[r]
                if rest:
                    turned = pltpu.roll(total, 8 - rest, 1)
                    total = jnp.where(row_in_lane < 8 - rest, turned[:blocks], turned[1:])
                mixed[r] = total if mixed[r] is None else mixed[r] + total
        for r in range(rows):
            mixed_ref[store_row + r, pl.ds(block, blocks), :, lanes] = mixed[r]
        return carry

    lax.fori_loop(0, 2 * chunks, step, 0)


def gelu_half(half):
    c = 2.0 * 0.7978845608028654
    inner = half * (c + (c * 4.0 * 0.044715) * (half * half))
    return half + half * jnp.tanh(inner)


def encoder(
    image, side, edge, w_patch, taps, gain_one, w_up, w_down, scale, gain_two, w_keys, w_values, query,
    out, embed, ordered, pixels, mixed, features, sums,
):
    rows = embed.shape[0] - 6
    columns = (embed.shape[1] - 2) * 8
    width = embed.shape[3]
    stem(image, side, edge, w_patch, embed, ordered, pixels)
    per_tile = TOKENS // columns
    tiles = rows // per_tile

    def block_step(tile, carry):
        row = tile * per_tile
        conv_tile(embed, taps, mixed, row, 0)
        normed = layer_norm(mixed[...].reshape(TOKENS, width), gain_one[...]).astype(BF16)
        down = None
        for start in range(0, w_up.shape[1], 256):
            hidden = gelu_half(matmul(normed, w_up[:, start : start + 256])).astype(BF16)
            part = matmul(hidden, w_down[start : start + 256, :])
            down = part if down is None else down + part
        center = embed[pl.ds(row + 3, per_tile), 1 : columns // 8 + 1].reshape(TOKENS, width)
        block = center + scale[...] * down
        features[pl.ds(pl.multiple_of(tile * TOKENS, TOKENS), TOKENS), :] = layer_norm(
            block, gain_two[...]
        ).astype(BF16)
        return carry

    lax.fori_loop(0, tiles, block_step, 0)
    pair = 2 * HEAD_DIM
    sums[...] = jnp.zeros_like(sums)
    latents = out.shape[2]
    lowest = jnp.full((1, 2 * latents), -jnp.inf, F32)
    start_stats = tuple((lowest, jnp.zeros((1, 2 * latents), F32)) for _ in range(HEADS // 2))

    def attend_step(tile, stats):
        feature = features[pl.ds(pl.multiple_of(tile * TOKENS, TOKENS), TOKENS), :]
        turned = feature.T
        result = []
        for p in range(HEADS // 2):
            top, total = stats[p]
            keys = matmul(feature, w_keys[:, p * pair : p * pair + pair]).astype(BF16)
            scores = matmul(keys, query[p])
            top_new = jnp.maximum(top, jnp.max(scores, axis=0, keepdims=True))
            expo = jnp.exp(scores - top_new)
            factor = jnp.exp(top - top_new)
            total = total * factor + jnp.sum(expo, axis=0, keepdims=True)
            lanes = slice(p * 2 * latents, (p + 1) * 2 * latents)
            sums[:, lanes] = sums[:, lanes] * factor + matmul(turned, expo.astype(BF16))
            result.append((top_new, total))
        return tuple(result)

    stats = lax.fori_loop(0, tiles, attend_step, start_stats)
    per_head = out.shape[0] // HEADS
    depth = HEAD_DIM // per_head
    for head in range(HEADS):
        lanes = slice(head * latents, (head + 1) * latents)
        mine = slice((head % 2) * latents, (head % 2 + 1) * latents)
        total_sums = sums[:, lanes]
        high = total_sums.astype(BF16)
        low = (total_sums - high.astype(F32)).astype(BF16)
        weights = w_values[:, head * HEAD_DIM : (head + 1) * HEAD_DIM]
        value = matmul(weights, high, ((0,), (0,))) + matmul(weights, low, ((0,), (0,)))
        lines = []
        for stat in stats[head // 2]:
            rest = stat[:, mine]
            for _ in range(3):
                piece = rest.astype(BF16).astype(F32)
                lines.append(piece)
                rest = rest - piece
        line = iota((16, latents), 0)
        extra = jnp.zeros((16, latents), F32)
        for k, piece in enumerate(lines):
            extra = jnp.where(line == k, piece, extra)
        for part in range(per_head):
            place = head * per_head + part
            out[place, :depth] = value[part * depth : (part + 1) * depth].astype(BF16)
            out[place, depth:] = extra.astype(BF16)


def split_three(value):
    high = lax.reduce_precision(value, 8, 7)
    rest = value - high
    middle = lax.reduce_precision(rest, 8, 7)
    return high, middle, rest - middle


def pack_partial(sums, top, total):
    rows = jnp.stack([*split_three(top), *split_three(total)], axis=-2)
    rows = jnp.pad(rows, ((0, 0),) * (rows.ndim - 2) + ((0, 10), (0, 0)))
    return jnp.concatenate([sums, rows], axis=-2).astype(BF16)


def merge_partials(packed):
    packed = packed.astype(F32)
    count = packed.shape[1] - 16
    stats = packed[:, count:]
    top = (stats[:, 0] + stats[:, 1]) + stats[:, 2]
    total = (stats[:, 3] + stats[:, 4]) + stats[:, 5]
    top_all = jnp.max(top, axis=0)
    factor = jnp.exp(top - top_all)
    sums = jnp.sum(packed[:, :count] * factor[:, None], axis=0)
    return sums, top_all, jnp.sum(total * factor, axis=0)


def share(value, axis):
    size = lax.axis_size(axis)
    return lax.all_to_all(jnp.broadcast_to(value, (size, *value.shape)), axis, 0, 0)


def partial_sums(
    image, side, edge, w_patch, dw_kernel, gain_one, w_up, w_down, scale_block, gain_two, w_kv, pairs, cols
):
    channels, height, breadth = image.shape
    tile_rows, tile_cols = height // 4, breadth // 4
    count, width = pairs.shape[2] // 2, w_patch.shape[1]
    kv_width = HEADS * HEAD_DIM
    taps = jnp.broadcast_to(dw_kernel.astype(F32).reshape(49, 1, width), (49, 8, width))
    return pl.pallas_call(
        encoder,
        out_shape=jax.ShapeDtypeStruct((cols, kv_width // cols + 16, count), BF16),
        in_specs=[pl.BlockSpec(memory_space=pltpu.VMEM)] * 13,
        out_specs=pl.BlockSpec(memory_space=pltpu.VMEM),
        scratch_shapes=[
            pltpu.VMEM((tile_rows + 6, tile_cols // 8 + 2, 8, width), F32),
            pltpu.VMEM(((tile_rows + 6) * 16, breadth + 128), BF16),
            pltpu.VMEM((4, (tile_rows + 6) * 16, tile_cols + 128), BF16),
            pltpu.VMEM((TOKENS // tile_cols, tile_cols // 8, 8, width), F32),
            pltpu.VMEM((tile_rows * tile_cols, width), BF16),
            pltpu.VMEM((width, HEADS * count), F32),
        ],
        compiler_params=pltpu.CompilerParams(vmem_limit_bytes=48 * 2**20),
        name="encoder",
    )(
        image.reshape(channels * height, breadth),
        side.reshape(channels * height, 128),
        edge.reshape(96, breadth + 128),
        w_patch,
        taps,
        gain_one.reshape(1, width),
        w_up * jnp.asarray(0.5, BF16),
        w_down,
        scale_block.reshape(1, width),
        gain_two.reshape(1, width),
        w_kv[:, :kv_width],
        w_kv[:, kv_width:],
        pairs,
    )


def body(
    image,
    w_patch,
    dw_kernel,
    gain_one,
    w_up,
    w_down,
    scale_block,
    gain_two,
    w_kv,
    latents,
    gain_three,
    w_q,
    w_o,
):
    channels, height = image.shape[:2]
    count = latents.shape[0]
    kv_width = HEADS * HEAD_DIM
    cols = lax.axis_size("cols")
    left, right = exchange(image, "cols", 2, 12)
    side = jnp.concatenate(
        [left, right, jnp.zeros((channels, height, 104), image.dtype)], axis=2
    )
    wide = jnp.concatenate([image, side], axis=2)
    above, below = exchange(wide, "rows", 1, 12)
    edge = jnp.pad(jnp.concatenate([above, below], axis=0), ((0, 0), (0, 4), (0, 0)))
    lat_norm = layer_norm(latents.astype(F32), gain_three).astype(BF16)
    query = (jnp.dot(lat_norm, w_q, preferred_element_type=F32) * HEAD_DIM ** (-0.5)).astype(BF16)
    heads = query.reshape(count, HEADS // 2, 2, HEAD_DIM).transpose(1, 2, 3, 0)
    pairs = jnp.einsum("pidl,ij->pidjl", heads, jnp.eye(2, dtype=BF16)).reshape(
        HEADS // 2, 2 * HEAD_DIM, 2 * count
    )
    packed = partial_sums(
        image, side, edge, w_patch, dw_kernel, gain_one, w_up, w_down, scale_block, gain_two, w_kv, pairs, cols
    )
    partial = merge_partials(lax.all_to_all(packed, "cols", 0, 0))
    sums, _, total = merge_partials(share(pack_partial(*partial), "rows"))
    attended = share((sums / total).astype(BF16), "cols").reshape(kv_width, -1)
    return latents.astype(F32) + matmul(attended, w_o, ((0,), (0,)))


def solution(mesh):
    in_specs = (P(None, "rows", "cols"), P(), P(), P(), P(), P(), P(), P(), P(), P(), P(), P(), P())
    out_specs = P()
    return jax.shard_map(body, mesh=mesh, in_specs=in_specs, out_specs=out_specs, check_vma=False)
```

time: 231 us -> 153 us (0.66)
  Pallas kernels: 0 us -> 54.8 us
  other arithmetic: 57.2 us -> 7.46 us
  matrix products: 41.8 us -> 4.31 us
  local copies, waits for them, and re-layouts: 49.7 us -> 12.3 us
  waiting for transfers between devices: 8.61 us -> 3.24 us
  starting transfers between devices: 16.9 us -> 12.6 us
    pallas_call x0 -> x1, Pallas kernels: none -> 54.8 us  [partial_sums(): pl.pallas_call(encoder, out_shape=jax.ShapeDtypeStruct((cols, kv_width //...]
    dot_general x7 -> x2, matrix products: 41.8 us -> 4.31 us  [the longest x1 2.86 us: matmul(): lax.dot_general(left, right, (dims, ((), ())), preferred_element_type=F32)]
    reduce_sum x2 -> x1, other arithmetic: 37.5 us -> 1.07 us  [layer_norm(): center = values - jnp.mean(values, axis=-1, keepdims=True)]
    reshape x1 -> x2, local copies, waits for them, and re-layouts: 28.9 us -> 1.54 us  [the longest x1 1.37 us: body(): jnp.einsum('pidl,ij->pidjl', heads, jnp.eye(2, dtype=BF16))]
    transpose x1, local copies, waits for them, and re-layouts: 10.5 us -> 0.2 us  [body(): heads = query.reshape(count, HEADS // 2, 2, HEAD_DIM).transpose(1, 2, 3, 0)]
    reduce_sum x1 -> x0, other arithmetic: 8.09 us -> none  [body(): total_local = jnp.sum(expo, axis=-1)]
    slice x5 -> x2, local copies, waits for them, and re-layouts: 9.64 us -> 2.65 us  [exchange(): lax.slice_in_dim(value, length - width, length, axis=dim)]
    ppermute x4, waiting for transfers between devices: 8.61 us -> 3.24 us  [the longest x2 3.23 us: exchange(): lax.ppermute(lax.slice_in_dim(value, 0, width, axis=dim), axis, down)]
  transfers between devices with their start and end apart: 4 -> 4, of which waited for: 3 -> 1; matrix products, arithmetic and copies ran while one was open for 0% -> 7% of each run, Pallas kernels for 0% -> 0%
where the time goes in v2:
time: 153 us; the launch traced here: 152 us
  blocking collectives  56.9 us (37%)
  Pallas kernels  54.8 us (36%)
  starting transfers between devices  12.6 us (8%)
  local copies, waits for them, and re-layouts  12.3 us (8%)
  other arithmetic  7.46 us (5%)
  matrix products  4.31 us (3%)
  waiting for transfers between devices  3.24 us (2%)
    pallas_call x1, Pallas kernels, partial_sums(): pl.pallas_call(encoder, out_shape=jax.ShapeDtypeStruct((cols, kv_width //...  54.8 us
    all_to_all x1, blocking collectives, body(): partial = merge_partials(lax.all_to_all(packed, 'cols', 0, 0))  28.9 us
    all_to_all x2, blocking collectives, share(): lax.all_to_all(jnp.broadcast_to(value, (size, *value.shape)), axis, 0, 0)  27.9 us
    ppermute x2, starting transfers between devices, exchange(): lax.ppermute(lax.slice_in_dim(value, length - width, length, axis=dim), a...  9.41 us
    unnamed x22, local copies, waits for them, and re-layouts  3.89 us
    ppermute x2, waiting for transfers between devices, exchange(): lax.ppermute(lax.slice_in_dim(value, 0, width, axis=dim), axis, down)  3.23 us
    ppermute x2, starting transfers between devices, exchange(): lax.ppermute(lax.slice_in_dim(value, 0, width, axis=dim), axis, down)  3.21 us
  transfers between devices with their start and end apart: 4, of which 1 were waited for; matrix products, arithmetic and copies ran while one was open for 7% of the time, Pallas kernels for 0%

profile of v2, /device:TPU:1, one launch (start us, length us, event | category | flops | bytes accessed | tf_op | source)
XLA Modules:
  0.0 151.8 jit_solution(11021371309947202424)
XLA Ops:
  0.0 0.0 copy-start
  0.0 1.7 %fusion.30 = (bf16[3,64,12]{2,1,0:T(8,128)(2,1)}, bf16[3,64,12]{2,1,0:T(8,128)(2,1)}) fusion(bf16[3,64,1024]{2,1,0:T(8,128)(2,1)} %param.13), kind=kLoop, calls=%fused_computation.62 | loop fusion | bytes 18432 | tf_op jit(solution)/shard_map/slice | solution.py:19
  1.7 6.3 %collective-permute-start = (bf16[3,64,12]{2,1,0:T(8,128)(2,1)}, bf16[3,64,12]{2,1,0:T(8,128)(2,1)}, u32[]{:S(2)}, u32[]{:S(2)}) collective-permute-start(bf16[3,64,12]{2,1,0:T(8,128)(2,1)} %get-tuple-element.16), channel_id=1, source_target_pairs={{0,1},{1,2},{2,3},{3,4},{4,5},{5,6},{6,7},{7,8},{8,9},{9,10},{10,1... | collective-permute-start | bytes 13832 | tf_op jit(solution)/shard_map/ppermute | solution.py:19
  8.0 1.9 %collective-permute-start.1 = (bf16[3,64,12]{2,1,0:T(8,128)(2,1)}, bf16[3,64,12]{2,1,0:T(8,128)(2,1)}, u32[]{:S(2)}, u32[]{:S(2)}) collective-permute-start(bf16[3,64,12]{2,1,0:T(8,128)(2,1)} %get-tuple-element.17), channel_id=1, source_target_pairs={{1,0},{2,1},{3,2},{4,3},{5,4},{6,5},{7,6},{8,7},{9,8},{10,9},{11,1... | collective-permute-start | bytes 13832 | tf_op jit(solution)/shard_map/ppermute | solution.py:20
  9.9 1.1 convert_reduce_fusion
  11.0 1.2 fusion.3
  12.2 0.0 copy-done
  12.2 1.4 fusion
  13.6 0.2 reshape.117
  13.8 0.2 copy.26
  14.0 0.0 copy-start.10
  14.0 0.0 copy-start.3
  14.0 2.5 %fusion.27 = (bf16[256,1024]{1,0:T(8,128)(2,1)S(1)}, bf16[256,1024]{1,0:T(8,128)(2,1)}, bf16[256,1024]{1,0:T(8,128)(2,1)}) fusion(bf16[256,2048]{1,0:T(8,128)(2,1)} %param.21, bf16[256,1024]{1,0:T(8,128)(2,1)} %param.17), kind=kLoop, calls=%fused_computation.59 | loop fusion | flops 262144 | bytes 3145728 | tf_op jit(solution)/shard_map/slice | solution.py:283
  16.5 0.0 copy-start.6
  16.5 0.0 copy-start.7
  16.5 1.4 multiply_bitcast_fusion
  17.9 0.0 copy-done.10
  17.9 0.6 reshape.120
  18.5 1.4 reshape.118.query
  19.9 0.0 collective-permute-done
  19.9 0.0 collective-permute-done.1
  19.9 0.6 broadcast_in_dim.13
  20.6 0.0 copy-done.3
  20.6 1.7 %concatenate.15 = bf16[3,64,1152]{2,1,0:T(8,128)(2,1)} concatenate(bf16[3,64,1024]{2,1,0:T(8,128)(2,1)S(1)} %copy-done.3, bf16[3,64,12]{2,1,0:T(8,128)(2,1)} %collective-permute-done, bf16[3,64,12]{2,1,0:T(8,128)(2,1)} %collective-permute-done.1, bf16[3,64,104]{2,1,0:T(8,128)(2,1)} %broadcast_in_dim.13), dimensions={2} | concatenate | bytes 884736 | tf_op jit(solution)/shard_map/concatenate | solution.py:311
  22.3 1.0 fusion.28
  23.3 3.1 %collective-permute-start.2 = (bf16[3,12,1152]{2,1,0:T(8,128)(2,1)S(1)}, bf16[3,12,1152]{2,1,0:T(8,128)(2,1)S(1)}, u32[]{:S(2)}, u32[]{:S(2)}) collective-permute-start(bf16[3,12,1152]{2,1,0:T(8,128)(2,1)S(1)} %get-tuple-element.11), channel_id=1, source_target_pairs={{0,32},{32,64},{64,96},{96,128},{128,160},{160,192},{192,224},{1,3... | collective-permute-start | bytes 248840 | tf_op jit(solution)/shard_map/ppermute | solution.py:19
  26.4 1.3 collective-permute-start.3
  27.7 0.9 pad_maximum_fusion
  28.7 0.0 collective-permute-done.2
  28.7 3.2 %collective-permute-done.3 = bf16[3,12,1152]{2,1,0:T(8,128)(2,1)S(1)} collective-permute-done((bf16[3,12,1152]{2,1,0:T(8,128)(2,1)S(1)}, bf16[3,12,1152]{2,1,0:T(8,128)(2,1)S(1)}, u32[]{:S(2)}, u32[]{:S(2)}) %collective-permute-start.3) | collective-permute-done | bytes 82976 | tf_op jit(solution)/shard_map/ppermute | solution.py:20
  32.0 0.8 broadcast_in_dim.30.taps
  32.8 0.0 copy-done.6
  32.8 0.0 copy-done.7
  32.8 0.0 copy-done.8
  32.8 0.0 copy-start.1
  32.8 1.0 copy-done.1
  33.9 1.0 copy-done.2
  34.9 1.0 copy-done.4
  36.0 0.7 copy-done.5
  36.7 54.8 %encoder.1 = bf16[32,48,128]{2,1,0:T(8,128)(2,1)S(1)} custom-call(bf16[192,1024]{1,0:T(8,128)(2,1)S(1)} %bitcast.55, bf16[192,128]{1,0:T(8,128)(2,1)S(1)} %bitcast.57, bf16[96,1152]{1,0:T(8,128)(2,1)S(1)} %bitcast.56, bf16[48,256]{1,0:T(8,128)(2,1)S(1)} %copy-done.5, f32[49,8,256]{2,1,0:T(8,128)S(1)} %broadcast_in_dim.30.taps, f32[1,256]{1,0:T(1,128)S(1)} %bitcast.58, ...), custom_call_target="tpu_custom_call" | custom-call | tf_op jit(solution)/shard_map/encoder/pallas_call | solution.py:256
  91.5 0.0 copy-start.9
  91.5 28.9 %all_to_all.15 = bf16[32,48,128]{2,1,0:T(8,128)(2,1)S(1)} all-to-all(bf16[32,48,128]{2,1,0:T(8,128)(2,1)S(1)} %encoder.1), channel_id=1, replica_groups=mesh['rows'=8,'cols'=32] {'cols'}, dimensions={0} | all-to-all | bytes 786432 | tf_op jit(solution)/shard_map/all_to_all | solution.py:323
  120.5 0.1 convert_element_type.29
  120.6 0.1 fusion.6
  120.8 10.4 %all_to_all.16 = bf16[8,48,128]{2,1,0:T(8,128)(2,1)S(1)} all-to-all(bf16[8,48,128]{2,1,0:T(8,128)(2,1)S(1)} %broadcast_in_dim.31), channel_id=1, replica_groups=mesh['rows'=8,'cols'=32] {'rows'}, dimensions={0} | all-to-all | bytes 196608 | tf_op jit(solution)/shard_map/all_to_all | solution.py:245
  131.3 17.6 %all_to_all.17 = bf16[32,32,128]{2,1,0:T(8,128)(2,1)S(1)} all-to-all(bf16[32,32,128]{2,1,0:T(8,128)(2,1)S(1)} %broadcast_in_dim.32), channel_id=1, replica_groups=mesh['rows'=8,'cols'=32] {'cols'}, dimensions={0} | all-to-all | bytes 524288 | tf_op jit(solution)/shard_map/all_to_all | solution.py:245
  148.9 0.0 copy-done.9
  148.9 2.9 %convolution_add_fusion = f32[128,1024]{1,0:T(8,128)} fusion(bf16[1024,128]{1,0:T(8,128)(2,1)S(1)} %bitcast.61, bf16[1024,1024]{1,0:T(8,128)(2,1)} %param.25, bf16[128,1024]{1,0:T(8,128)(2,1)S(1)} %copy-done.9), kind=kOutput, calls=%fused_computation | convolution fusion | flops 268697600 | bytes 3145728 | tf_op jit(solution)/shard_map/dot_general | solution.py:31
  (27 shorter events, 0.4 us)
Async XLA Ops:
  0.0 12.2 %copy-start = (bf16[1024,1024]{1,0:T(8,128)(2,1)S(1)}, bf16[1024,1024]{1,0:T(8,128)(2,1)}, u32[]{:S(2)}) copy-start(bf16[1024,1024]{1,0:T(8,128)(2,1)} %param.24) | copy-start | bytes 6291460
  1.7 18.2 %collective-permute-start = (bf16[3,64,12]{2,1,0:T(8,128)(2,1)}, bf16[3,64,12]{2,1,0:T(8,128)(2,1)}, u32[]{:S(2)}, u32[]{:S(2)}) collective-permute-start(bf16[3,64,12]{2,1,0:T(8,128)(2,1)} %get-tuple-element.16), channel_id=1, source_target_pairs={{0,1},{1,2},{2,3},{3,4},{4,5},{5,6},{6,7},{7,8},{8,9},{9,10},{10,1... | collective-permute-start | bytes 13832 | tf_op jit(solution)/shard_map/ppermute | solution.py:19
  8.0 12.0 %collective-permute-start.1 = (bf16[3,64,12]{2,1,0:T(8,128)(2,1)}, bf16[3,64,12]{2,1,0:T(8,128)(2,1)}, u32[]{:S(2)}, u32[]{:S(2)}) collective-permute-start(bf16[3,64,12]{2,1,0:T(8,128)(2,1)} %get-tuple-element.17), channel_id=1, source_target_pairs={{1,0},{2,1},{3,2},{4,3},{5,4},{6,5},{7,6},{8,7},{9,8},{10,9},{11,1... | collective-permute-start | bytes 13832 | tf_op jit(solution)/shard_map/ppermute | solution.py:20
  14.0 3.9 %copy-start.10 = (bf16[7,7,256]{2,1,0:T(8,128)(2,1)S(1)}, bf16[7,7,256]{2,1,0:T(8,128)(2,1)}, u32[]{:S(2)}) copy-start(bf16[7,7,256]{2,1,0:T(8,128)(2,1)} %param.15) | copy-start | bytes 75268
  14.0 6.5 %copy-start.3 = (bf16[3,64,1024]{2,1,0:T(8,128)(2,1)S(1)}, bf16[3,64,1024]{2,1,0:T(8,128)(2,1)}, u32[]{:S(2)}) copy-start(bf16[3,64,1024]{2,1,0:T(8,128)(2,1)} %param.13) | copy-start | bytes 1179652
  16.5 16.3 %copy-start.6 = (f32[256]{0:T(256)S(1)}, f32[256]{0:T(256)}, u32[]{:S(2)}) copy-start(f32[256]{0:T(256)} %param.16) | copy-start | bytes 3076
  16.5 16.3 %copy-start.7 = (f32[256]{0:T(256)S(1)}, f32[256]{0:T(256)}, u32[]{:S(2)}) copy-start(f32[256]{0:T(256)} %param.19) | copy-start | bytes 3076
  16.5 16.3 %copy-start.8 = (f32[256]{0:T(256)S(1)}, f32[256]{0:T(256)}, u32[]{:S(2)}) copy-start(f32[256]{0:T(256)} %param.20) | copy-start | bytes 3076
  23.3 5.4 %collective-permute-start.2 = (bf16[3,12,1152]{2,1,0:T(8,128)(2,1)S(1)}, bf16[3,12,1152]{2,1,0:T(8,128)(2,1)S(1)}, u32[]{:S(2)}, u32[]{:S(2)}) collective-permute-start(bf16[3,12,1152]{2,1,0:T(8,128)(2,1)S(1)} %get-tuple-element.11), channel_id=1, source_target_pairs={{0,32},{32,64},{64,96},{96,128},{128,160},{160,192},{192,224},{1,3... | collective-permute-start | bytes 248840 | tf_op jit(solution)/shard_map/ppermute | solution.py:19
  26.4 5.5 %collective-permute-start.3 = (bf16[3,12,1152]{2,1,0:T(8,128)(2,1)S(1)}, bf16[3,12,1152]{2,1,0:T(8,128)(2,1)S(1)}, u32[]{:S(2)}, u32[]{:S(2)}) collective-permute-start(bf16[3,12,1152]{2,1,0:T(8,128)(2,1)S(1)} %get-tuple-element.12), channel_id=1, source_target_pairs={{32,0},{64,32},{96,64},{128,96},{160,128},{192,160},{224,192},{33,... | collective-permute-start | bytes 248840 | tf_op jit(solution)/shard_map/ppermute | solution.py:20
  32.8 1.0 copy-start.1
  33.9 1.0 copy-start.2
  34.9 1.0 copy-start.4
  36.0 0.7 copy-start.5
  91.5 57.4 %copy-start.9 = (bf16[128,1024]{1,0:T(8,128)(2,1)S(1)}, bf16[128,1024]{1,0:T(8,128)(2,1)}, u32[]{:S(2)}) copy-start(bf16[128,1024]{1,0:T(8,128)(2,1)} %param.22) | copy-start | bytes 786436

commit v3 on v2

v3 whole, which is shorter than its diff:
```python
import jax
import jax.numpy as jnp
from jax import lax
from jax.experimental import pallas as pl
from jax.experimental.pallas import tpu as pltpu
from jax.sharding import PartitionSpec as P

HEADS = 8
HEAD_DIM = 128
F32 = jnp.float32
BF16 = jnp.bfloat16
TOKENS = 1024
ATTEND = 1024
CONV_ROWS = 4
CONV_BLOCKS = 1
STEM = 11


def exchange(last, first, axis):
    devices = lax.axis_size(axis)
    up = [(i, i + 1) for i in range(devices - 1)]
    down = [(j, i) for i, j in up]
    return lax.ppermute(last, axis, up), lax.ppermute(first, axis, down)


def layer_norm(values, gain):
    center = values - jnp.mean(values, axis=-1, keepdims=True)
    spread = jnp.mean(center * center, axis=-1, keepdims=True)
    return center * lax.rsqrt(spread + 1e-06) * gain


def matmul(left, right, dims=((1,), (0,))):
    return lax.dot_general(left, right, (dims, ((), ())), preferred_element_type=F32)


def iota(shape, dim):
    return lax.broadcasted_iota(jnp.int32, shape, dim)


def ones_where(mask):
    return jnp.where(mask, 1.0, 0.0).astype(BF16)


SPREAD = (
    (1, 0, -5.25, 0, 5.25, 0, -1, 0),
    (0, 1, 1, -4.25, -4.25, 1, 1, 0),
    (0, -1, 1, 4.25, -4.25, -1, 1, 0),
    (0, 0.5, 0.25, -2.5, -1.25, 2, 1, 0),
    (0, -0.5, 0.25, 2.5, -1.25, -2, 1, 0),
    (0, 2, 4, -2.5, -5, 0.5, 1, 0),
    (0, -2, 4, 2.5, -5, -0.5, 1, 0),
    (0, -1, 0, 5.25, 0, -5.25, 0, 1),
)
POINTS = (0, 1, -1, 2, -2, 0.5, -0.5)
SCALE = (1, -2 / 9, -2 / 9, 1 / 90, 1 / 90, 32 / 45, 32 / 45, 1)


def stem(image, left, right, above, below, w_patch, dw_kernel, spread, taps, ordered, pixels, split):
    rows = spread.shape[0]
    local = (rows - 6) * 4
    places = rows * 16

    def pick_rows(count, first, wanted_of):
        place, source = iota((places, count), 0), iota((places, count), 1)
        slot = place % 16
        pixel_row = (place // 16) * 4 + slot % 4 - first
        return ones_where((slot < 12) & wanted_of(source, slot // 4, pixel_row))

    pick = pick_rows(
        3 * local, 12, lambda s, c, r: (r >= 0) & (r < local) & (s == c * local + r)
    )
    pick_above = pick_rows(48, -4, lambda s, c, r: (r < 16) & (s == c * 16 + r))
    pick_below = pick_rows(48, 12 + local, lambda s, c, r: (r >= 0) & (s == c * 16 + r))
    width = image.shape[1]
    for source, base in ((image, 0), (left, width), (right, width + 128)):
        step = min(256, source.shape[1])
        for start in range(0, source.shape[1], step):
            lanes = slice(base + start, base + start + step)
            ordered[:, lanes] = (
                matmul(pick, source[:, start : start + step])
                + matmul(pick_above, above[:, lanes])
                + matmul(pick_below, below[:, lanes])
            ).astype(BF16)
    for tile in range(pixels.shape[2] // 128):
        low = max(0, 512 * tile - 32) // 128 * 128
        high = min(width, 512 * tile + 512)
        parts = [(low, high, low)]
        if 512 * tile < 32:
            parts.append((width, width + 128, -128))
        if 512 * tile + 480 > width:
            parts.append((width + 128, width + 256, width))
        found = None
        for begin, end, first in parts:
            lane, source = iota((end - begin, 512), 1), iota((end - begin, 512), 0)
            wanted = 4 * (tile * 128 + lane % 128 - 8) + lane // 128
            part = matmul(ordered[:, begin:end], ones_where(source + first == wanted))
            found = part if found is None else found + part
        found = found.astype(BF16)
        for phase in range(4):
            pixels[phase, :, tile * 128 : tile * 128 + 128] = found[:, phase * 128 : phase * 128 + 128]
    place, source = iota((64, 48), 0), iota((64, 48), 1)
    slot = place % 16
    pick = ones_where((slot < 12) & (source == slot * 4 + place // 16))
    weights = matmul(pick, w_patch[...]).astype(BF16)
    offset = iota((64, 144), 1) - 5 - 2 * iota((64, 144), 0)
    for point in range(8):
        value = jnp.zeros((64, 144), F32)
        for m in range(8):
            if SPREAD[point][m]:
                value = jnp.where(offset == m, float(SPREAD[point][m]), value)
        split[point * 64 : point * 64 + 64] = value.astype(BF16)
    for parity in range(2):
        split[512 + parity * 64 : 576 + parity * 64] = ones_where(offset == 3 + parity)
    place, source = iota((16, 7), 0), iota((16, 7), 1)
    powers = jnp.zeros((16, 7), F32)
    for point in range(8):
        for j in range(7):
            weight = float(POINTS[point] ** j) if point < 7 else float(j == 6)
            if weight:
                powers = jnp.where((place == point) & (source == j), weight, powers)
    for i in range(7):
        value = matmul(powers.astype(BF16), dw_kernel[i])
        for point in range(8):
            taps[point, i] = jnp.broadcast_to(value[point : point + 1] * SCALE[point], taps.shape[2:])

    def step(row, carry):
        patches = jnp.concatenate(
            [pixels[phase, pl.ds(pl.multiple_of(row * 16, 16), 16), :] for phase in range(4)], axis=0
        )
        value = matmul(patches, weights, ((0,), (0,))).astype(BF16)
        for half in range(2):
            found = matmul(split[...], value[half * 128 : half * 128 + 144])
            spread[row, half] = found.reshape(spread.shape[2:])
        return carry

    lax.fori_loop(0, rows, step, 0, unroll=STEM)


def conv_tile(spread, taps, mixed, row, rows, blocks):
    chunks = 8 // blocks

    def step(index, carry):
        half = index // chunks
        block = pl.ds((index % chunks) * blocks, blocks)
        for start in range(0, spread.shape[5], 128):
            lanes = slice(start, start + 128)

            def products(point):
                sums = [None] * rows
                weights = [taps[point, i, :, lanes] for i in range(7)]
                for line in range(rows + 6):
                    value = spread[row + line, half, point, block, :, lanes]
                    for r in range(rows):
                        if 0 <= line - r < 7:
                            term = value * weights[line - r]
                            sums[r] = term if sums[r] is None else sums[r] + term
                return sums

            even, odd = products(0), products(7)
            for point, factor in ((1, 1.0), (3, 2.0), (5, 0.5)):
                plus, minus = products(point), products(point + 1)
                for r in range(rows):
                    even[r] = even[r] + (plus[r] + minus[r])
                    gap = plus[r] - minus[r]
                    odd[r] = odd[r] + (gap if factor == 1.0 else gap * factor)
            for r in range(rows):
                mixed[r, half, 0, block, :, lanes] = even[r]
                mixed[r, half, 1, block, :, lanes] = odd[r]
        return carry

    lax.fori_loop(0, 2 * chunks, step, 0)


def gelu_half(half):
    c = 2.0 * 0.7978845608028654
    inner = half * (c + (c * 4.0 * 0.044715) * (half * half))
    return half + half * jnp.tanh(inner)


def encoder(
    image, left, right, above, below, w_patch, dw_kernel, gain_one, scale, gain_two, query,
    w_up_far, w_down_far, w_kv_far,
    out, spread, taps, ordered, pixels, split, mixed, features, sums, w_up, w_down, w_kv, arrived,
):
    width = spread.shape[5]
    tokens = features.shape[0]
    copies = [
        pltpu.make_async_copy(far, near, arrived.at[k])
        for k, (far, near) in enumerate(((w_up_far, w_up), (w_down_far, w_down), (w_kv_far, w_kv)))
    ]
    for copy in copies:
        copy.start()
    stem(
        image, left, right, above, below, w_patch, dw_kernel, spread, taps, ordered, pixels, split
    )
    for copy in copies:
        copy.wait()
    w_up[...] = w_up[...] * jnp.asarray(0.5, BF16)
    per_tile = mixed.shape[0]
    tiles = tokens // TOKENS

    def block_step(tile, carry):
        row = tile * per_tile
        conv_tile(spread, taps, mixed, row, CONV_ROWS, CONV_BLOCKS)
        normed = layer_norm(mixed[...].reshape(TOKENS, width), gain_one[...]).astype(BF16)
        down = None
        for start in range(0, w_up.shape[1], 256):
            hidden = gelu_half(matmul(normed, w_up[:, start : start + 256])).astype(BF16)
            part = matmul(hidden, w_down[start : start + 256, :])
            down = part if down is None else down + part
        center = spread[pl.ds(row + 3, per_tile), :, 8:10].reshape(TOKENS, width)
        block = center + scale[...] * down
        features[pl.ds(pl.multiple_of(tile * TOKENS, TOKENS), TOKENS), :] = layer_norm(
            block, gain_two[...]
        ).astype(BF16)
        return carry

    lax.fori_loop(0, tiles, block_step, 0)
    pair = 2 * HEAD_DIM
    sums[...] = jnp.zeros_like(sums)
    latents = out.shape[2]
    lowest = jnp.full((1, 2 * latents), -jnp.inf, F32)
    start_stats = tuple((lowest, jnp.zeros((1, 2 * latents), F32)) for _ in range(HEADS // 2))

    def attend_step(tile, stats):
        feature = features[pl.ds(pl.multiple_of(tile * ATTEND, ATTEND), ATTEND), :]
        turned = feature.T
        result = []

        def score(p):
            keys = matmul(feature, w_kv[:, p * pair : p * pair + pair]).astype(BF16)
            return matmul(keys, query[p])

        ahead = score(0)
        for p in range(HEADS // 2):
            top, total = stats[p]
            scores = ahead
            if p + 1 < HEADS // 2:
                ahead = score(p + 1)
            top_new = jnp.maximum(top, jnp.max(scores, axis=0, keepdims=True))
            expo = jnp.exp(scores - top_new)
            factor = jnp.exp(top - top_new)
            total = total * factor + jnp.sum(expo, axis=0, keepdims=True)
            lanes = slice(p * 2 * latents, (p + 1) * 2 * latents)
            sums[:, lanes] = sums[:, lanes] * factor + matmul(turned, expo.astype(BF16))
            result.append((top_new, total))
        return tuple(result)

    stats = lax.fori_loop(0, tokens // ATTEND, attend_step, start_stats)
    per_head = out.shape[0] // HEADS
    depth = HEAD_DIM // per_head
    for head in range(HEADS):
        lanes = slice(head * latents, (head + 1) * latents)
        mine = slice((head % 2) * latents, (head % 2 + 1) * latents)
        total_sums = sums[:, lanes]
        high = total_sums.astype(BF16)
        low = (total_sums - high.astype(F32)).astype(BF16)
        first = HEADS * HEAD_DIM + head * HEAD_DIM
        weights = w_kv[:, first : first + HEAD_DIM]
        value = matmul(weights, high, ((0,), (0,))) + matmul(weights, low, ((0,), (0,)))
        lines = []
        for stat in stats[head // 2]:
            rest = stat[:, mine]
            for _ in range(3):
                piece = rest.astype(BF16).astype(F32)
                lines.append(piece)
                rest = rest - piece
        line = iota((16, latents), 0)
        extra = jnp.zeros((16, latents), F32)
        for k, piece in enumerate(lines):
            extra = jnp.where(line == k, piece, extra)
        for part in range(per_head):
            place = head * per_head + part
            out[place, :depth] = value[part * depth : (part + 1) * depth].astype(BF16)
            out[place, depth:] = extra.astype(BF16)


def split_three(value):
    high = lax.reduce_precision(value, 8, 7)
    rest = value - high
    middle = lax.reduce_precision(rest, 8, 7)
    return high, middle, rest - middle


def pack_partial(sums, top, total):
    rows = jnp.stack([*split_three(top), *split_three(total)], axis=-2)
    rows = jnp.pad(rows, ((0, 0),) * (rows.ndim - 2) + ((0, 10), (0, 0)))
    return jnp.concatenate([sums, rows], axis=-2).astype(BF16)


def merge_partials(packed):
    packed = packed.astype(F32)
    count = packed.shape[1] - 16
    stats = packed[:, count:]
    top = (stats[:, 0] + stats[:, 1]) + stats[:, 2]
    total = (stats[:, 3] + stats[:, 4]) + stats[:, 5]
    top_all = jnp.max(top, axis=0)
    factor = jnp.exp(top - top_all)
    sums = jnp.sum(packed[:, :count] * factor[:, None], axis=0)
    return sums, top_all, jnp.sum(total * factor, axis=0)


def share(value, axis):
    size = lax.axis_size(axis)
    return lax.all_to_all(jnp.broadcast_to(value, (size, *value.shape)), axis, 0, 0)


def queries(latents, gain, w_q, out):
    count = latents.shape[0]
    normed = layer_norm(latents[...].astype(F32), gain[...]).astype(BF16)
    for head in range(HEADS):
        lanes = slice(head * HEAD_DIM, (head + 1) * HEAD_DIM)
        query = (matmul(normed, w_q[:, lanes]) * HEAD_DIM ** (-0.5)).astype(BF16)
        turned = query.astype(F32).T.astype(BF16)
        empty = jnp.zeros((HEAD_DIM, count), BF16)
        rows = slice((head % 2) * HEAD_DIM, (head % 2 + 1) * HEAD_DIM)
        out[head // 2, rows, :count] = turned if head % 2 == 0 else empty
        out[head // 2, rows, count:] = empty if head % 2 == 0 else turned


def paired_queries(latents, gain_three, w_q):
    count, width = latents.shape
    return pl.pallas_call(
        queries,
        out_shape=jax.ShapeDtypeStruct((HEADS // 2, 2 * HEAD_DIM, 2 * count), BF16),
        in_specs=[pl.BlockSpec(memory_space=pltpu.VMEM)] * 3,
        out_specs=pl.BlockSpec(memory_space=pltpu.VMEM),
        cost_estimate=pl.CostEstimate(
            flops=2 * count * width * w_q.shape[1], bytes_accessed=2 * w_q.size, transcendentals=0
        ),
        name="queries",
    )(latents, gain_three.reshape(1, width), w_q)


def partial_sums(
    image, left, right, above, below, w_patch, dw_kernel, gain_one, w_up, w_down, scale_block, gain_two,
    w_kv, pairs, cols,
):
    channels, height, breadth = image.shape
    tile_rows, tile_cols = height // 4, breadth // 4
    count, width = pairs.shape[2] // 2, w_patch.shape[1]
    return pl.pallas_call(
        encoder,
        out_shape=jax.ShapeDtypeStruct((cols, HEADS * HEAD_DIM // cols + 16, count), BF16),
        in_specs=[pl.BlockSpec(memory_space=pltpu.VMEM)] * 11 + [pl.BlockSpec(memory_space=pl.ANY)] * 3,
        out_specs=pl.BlockSpec(memory_space=pltpu.VMEM),
        scratch_shapes=[
            pltpu.VMEM((tile_rows + 6, 2, 10, 8, 8, width), F32),
            pltpu.VMEM((8, 7, 8, width), F32),
            pltpu.VMEM(((tile_rows + 6) * 16, breadth + 256), BF16),
            pltpu.VMEM((4, (tile_rows + 6) * 16, tile_cols + 128), BF16),
            pltpu.VMEM((640, 144), BF16),
            pltpu.VMEM((TOKENS // tile_cols, 2, 2, 8, 8, width), F32),
            pltpu.VMEM((tile_rows * tile_cols, width), BF16),
            pltpu.VMEM((width, HEADS * count), F32),
            pltpu.VMEM(w_up.shape, BF16),
            pltpu.VMEM(w_down.shape, BF16),
            pltpu.VMEM(w_kv.shape, BF16),
            pltpu.SemaphoreType.DMA((3,)),
        ],
        compiler_params=pltpu.CompilerParams(vmem_limit_bytes=52 * 2**20),
        name="encoder",
    )(
        image.reshape(channels * height, breadth),
        left.reshape(channels * height, 128),
        right.reshape(channels * height, 128),
        above.reshape(channels * 16, breadth + 256),
        below.reshape(channels * 16, breadth + 256),
        w_patch,
        dw_kernel,
        gain_one.reshape(1, width),
        scale_block.reshape(1, width),
        gain_two.reshape(1, width),
        pairs,
        w_up,
        w_down,
        w_kv,
    )


def project(attended, w_o, latents, out):
    out[...] = latents[...].astype(F32) + matmul(attended[...], w_o[...], ((0,), (0,)))


def body(
    image,
    w_patch,
    dw_kernel,
    gain_one,
    w_up,
    w_down,
    scale_block,
    gain_two,
    w_kv,
    latents,
    gain_three,
    w_q,
    w_o,
):
    cols = lax.axis_size("cols")
    left, right = exchange(image[:, :, -128:], image[:, :, :128], "cols")
    above, below = exchange(
        *(
            jnp.concatenate([image[:, rows], left[:, rows], right[:, rows]], axis=2)
            for rows in (slice(-16, None), slice(0, 16))
        ),
        "rows",
    )
    pairs = paired_queries(latents, gain_three, w_q)
    packed = partial_sums(
        image, left, right, above, below, w_patch, dw_kernel, gain_one, w_up, w_down, scale_block,
        gain_two, w_kv, pairs, cols,
    )
    partial = merge_partials(lax.all_to_all(packed, "cols", 0, 0))
    sums, _, total = merge_partials(share(pack_partial(*partial), "rows"))
    attended = share((sums / total).astype(BF16), "cols").reshape(HEADS * HEAD_DIM, -1)
    return pl.pallas_call(
        project,
        out_shape=jax.ShapeDtypeStruct(latents.shape, F32),
        in_specs=[pl.BlockSpec(memory_space=pltpu.VMEM)] * 3,
        out_specs=pl.BlockSpec(memory_space=pltpu.VMEM),
        name="project",
    )(attended, w_o, latents)


def solution(mesh):
    in_specs = (P(None, "rows", "cols"), P(), P(), P(), P(), P(), P(), P(), P(), P(), P(), P(), P())
    out_specs = P()
    return jax.shard_map(body, mesh=mesh, in_specs=in_specs, out_specs=out_specs, check_vma=False)
```

time: 153 us -> 127 us (0.83)
  local copies, waits for them, and re-layouts: 12.3 us -> 3.04 us
  other arithmetic: 7.46 us -> 0.38 us
  matrix products: 4.31 us -> 0 us
  Pallas kernels: 54.8 us -> 51.5 us
  waiting for transfers between devices: 3.24 us -> 0.94 us
    dot_general x2 -> x0, matrix products: 4.31 us -> none  [the longest x1 2.86 us: matmul(): lax.dot_general(left, right, (dims, ((), ())), preferred_element_type=F32)]
    pallas_call x1 -> x3, Pallas kernels: 54.8 us -> 51.5 us  [the longest x1 45.1 us: partial_sums(): pl.pallas_call(encoder, out_shape=jax.ShapeDtypeStruct((cols, HEADS * HEA...]
    unnamed x22 -> x14, local copies, waits for them, and re-layouts: 3.89 us -> 1.06 us
    slice x1 -> x0, other arithmetic: 2.47 us -> none  [partial_sums(): w_kv[:, kv_width:]]
    ppermute x4, waiting for transfers between devices: 3.24 us -> 0.94 us  [exchange(): return (lax.ppermute(last, axis, up), lax.ppermute(first, axis, down))]
    reduce_sum x2 -> x0, other arithmetic: 2.24 us -> none  [the longest x1 1.17 us: layer_norm(): spread = jnp.mean(center * center, axis=-1, keepdims=True)]
    broadcast_in_dim x3 -> x0, local copies, waits for them, and re-layouts: 2.12 us -> none  [the longest x2 1.49 us: partial_sums(): jnp.broadcast_to(dw_kernel.astype(F32).reshape(49, 1, width), (49, 8, wid...]
    concatenate x1 -> x0, local copies, waits for them, and re-layouts: 1.73 us -> none  [body(): wide = jnp.concatenate([image, side], axis=2)]
  transfers between devices with their start and end apart: 4 -> 4, of which waited for: 1 -> 2; matrix products, arithmetic and copies ran while one was open for 7% -> 1% of each run, Pallas kernels for 0% -> 3%
where the time goes in v3:
time: 127 us
  blocking collectives  57.9 us (46%)
  Pallas kernels  51.5 us (41%)
  starting transfers between devices  12.6 us (10%)
  local copies, waits for them, and re-layouts  3.04 us (2%)
    pallas_call x1, Pallas kernels, partial_sums(): pl.pallas_call(encoder, out_shape=jax.ShapeDtypeStruct((cols, HEADS * HEA...  45.1 us
    all_to_all x1, blocking collectives, body(): partial = merge_partials(lax.all_to_all(packed, 'cols', 0, 0))  29.5 us
    all_to_all x2, blocking collectives, share(): lax.all_to_all(jnp.broadcast_to(value, (size, *value.shape)), axis, 0, 0)  28.5 us
    ppermute x4, starting transfers between devices, exchange(): return (lax.ppermute(last, axis, up), lax.ppermute(first, axis, down))  12.6 us
    pallas_call x1, Pallas kernels, paired_queries(): pl.pallas_call(queries, out_shape=jax.ShapeDtypeStruct((HEADS // 2, 2 * H...  3.55 us
    pallas_call x1, Pallas kernels, body(): pl.pallas_call(project, out_shape=jax.ShapeDtypeStruct(latents.shape, F32...  2.92 us
  transfers between devices with their start and end apart: 4, of which 2 were waited for; matrix products, arithmetic and copies ran while one was open for 1% of the time, Pallas kernels for 3%

profile of v3, /device:TPU:1, one launch (start us, length us, event | category | flops | bytes accessed | tf_op | source)
XLA Modules:
  0.0 126.7 jit_solution(15290818615441862830)
XLA Ops:
  0.0 0.0 copy-start.1
  0.0 0.0 copy-start.6
  0.0 0.0 copy-start.5
  0.0 0.0 copy-start.4
  0.0 0.0 copy-start.2
  0.0 0.0 copy-start.3
  0.0 0.9 fusion.16
  0.9 5.1 %collective-permute-start.1 = (bf16[3,64,128]{2,1,0:T(8,128)(2,1)S(1)}, bf16[3,64,128]{2,1,0:T(8,128)(2,1)S(1)}, u32[]{:S(2)}, u32[]{:S(2)}) collective-permute-start(bf16[3,64,128]{2,1,0:T(8,128)(2,1)S(1)} %get-tuple-element.14), channel_id=1, source_target_pairs={{1,0},{2,1},{3,2},{4,3},{5,4},{6,5},{7,6},{8,7},{9,8},{10,9},{11,1... | collective-permute-start | bytes 147464 | tf_op jit(solution)/shard_map/ppermute | solution.py:23
  6.0 3.1 %collective-permute-start = (bf16[3,64,128]{2,1,0:T(8,128)(2,1)S(1)}, bf16[3,64,128]{2,1,0:T(8,128)(2,1)S(1)}, u32[]{:S(2)}, u32[]{:S(2)}) collective-permute-start(bf16[3,64,128]{2,1,0:T(8,128)(2,1)S(1)} %get-tuple-element.15), channel_id=1, source_target_pairs={{0,1},{1,2},{2,3},{3,4},{4,5},{5,6},{6,7},{7,8},{8,9},{9,10},{10,1... | collective-permute-start | bytes 147464 | tf_op jit(solution)/shard_map/ppermute | solution.py:23
  9.1 1.0 fusion.15
  10.1 0.0 collective-permute-done.1
  10.1 0.2 collective-permute-done
  10.3 3.1 %collective-permute-start.2 = (bf16[3,16,1280]{2,1,0:T(8,128)(2,1)S(1)}, bf16[3,16,1280]{2,1,0:T(8,128)(2,1)S(1)}, u32[]{:S(2)}, u32[]{:S(2)}) collective-permute-start(bf16[3,16,1280]{2,1,0:T(8,128)(2,1)S(1)} %pad_maximum_fusion), channel_id=1, source_target_pairs={{0,32},{32,64},{64,96},{96,128},{128,160},{160,192},{192,224},{1,3... | collective-permute-start | bytes 368648 | tf_op jit(solution)/shard_map/ppermute | solution.py:23
  13.5 1.3 %collective-permute-start.3 = (bf16[3,16,1280]{2,1,0:T(8,128)(2,1)S(1)}, bf16[3,16,1280]{2,1,0:T(8,128)(2,1)S(1)}, u32[]{:S(2)}, u32[]{:S(2)}) collective-permute-start(bf16[3,16,1280]{2,1,0:T(8,128)(2,1)S(1)} %pad_maximum_fusion.1), channel_id=1, source_target_pairs={{32,0},{64,32},{96,64},{128,96},{160,128},{192,160},{224,192},{33,... | collective-permute-start | bytes 368648 | tf_op jit(solution)/shard_map/ppermute | solution.py:23
  14.8 3.6 %queries.1.query = bf16[4,256,256]{2,1,0:T(8,128)(2,1)} custom-call(bf16[128,1024]{1,0:T(8,128)(2,1)} %latents.3, f32[1,1024]{1,0:T(1,128)} %bitcast.69, bf16[1024,1024]{1,0:T(8,128)(2,1)} %w_q.1), custom_call_target="tpu_custom_call" | custom-call | flops 268435456 | bytes 2097152 | tf_op jit(solution)/shard_map/queries/pallas_call | solution.py:323
  18.3 0.0 collective-permute-done.2
  18.3 0.8 collective-permute-done.3
  19.1 0.0 copy-done.1
  19.1 0.0 copy-done.6
  19.1 0.0 copy-done.5
  19.1 0.0 copy-done.4
  19.1 0.0 copy-done.2
  19.1 0.0 copy-done.3
  19.1 0.0 copy-start
  19.1 1.0 copy-done
  20.2 45.1 %encoder.1 = bf16[32,48,128]{2,1,0:T(8,128)(2,1)S(1)} custom-call(bf16[192,1024]{1,0:T(8,128)(2,1)S(1)} %bitcast.52, bf16[192,128]{1,0:T(8,128)(2,1)S(1)} %bitcast.56, bf16[192,128]{1,0:T(8,128)(2,1)S(1)} %bitcast.55, bf16[48,1280]{1,0:T(8,128)(2,1)S(1)} %bitcast.53, bf16[48,1280]{1,0:T(8,128)(2,1)S(1)} %bitcast.54, bf16[48,256]{1,0:T(8,128)(2,1)S(1)} %copy-done.3, ...), custom_call_target="tpu_custom_call" | custom-call | tf_op jit(solution)/shard_map/encoder/pallas_call | solution.py:342
  65.2 29.5 %all_to_all.15 = bf16[32,48,128]{2,1,0:T(8,128)(2,1)S(1)} all-to-all(bf16[32,48,128]{2,1,0:T(8,128)(2,1)S(1)} %encoder.1), channel_id=1, replica_groups=mesh['rows'=8,'cols'=32] {'cols'}, dimensions={0} | all-to-all | bytes 786432 | tf_op jit(solution)/shard_map/all_to_all | solution.py:414
  94.7 0.1 convert_element_type.12
  94.9 0.1 fusion
  95.1 10.4 %all_to_all.16 = bf16[8,48,128]{2,1,0:T(8,128)(2,1)S(1)} all-to-all(bf16[8,48,128]{2,1,0:T(8,128)(2,1)S(1)} %broadcast_in_dim.4), channel_id=1, replica_groups=mesh['rows'=8,'cols'=32] {'rows'}, dimensions={0} | all-to-all | bytes 196608 | tf_op jit(solution)/shard_map/all_to_all | solution.py:305
  105.7 18.1 %all_to_all.17 = bf16[32,32,128]{2,1,0:T(8,128)(2,1)} all-to-all(bf16[32,32,128]{2,1,0:T(8,128)(2,1)S(1)} %broadcast_in_dim.5), channel_id=1, replica_groups=mesh['rows'=8,'cols'=32] {'cols'}, dimensions={0} | all-to-all | bytes 524288 | tf_op jit(solution)/shard_map/all_to_all | solution.py:305
  123.7 2.9 %project.1 = f32[128,1024]{1,0:T(8,128)} custom-call(bf16[1024,128]{1,0:T(8,128)(2,1)} %bitcast.60, bf16[1024,1024]{1,0:T(8,128)(2,1)} %w_o.1, bf16[128,1024]{1,0:T(8,128)(2,1)} %latents.3), custom_call_target="tpu_custom_call" | custom-call | tf_op jit(solution)/shard_map/project/pallas_call | solution.py:417
  (22 shorter events, 0.4 us)
Async XLA Ops:
  0.0 19.1 %copy-start.1 = (bf16[3,64,1024]{2,1,0:T(8,128)(2,1)S(1)}, bf16[3,64,1024]{2,1,0:T(8,128)(2,1)}, u32[]{:S(2)}) copy-start(bf16[3,64,1024]{2,1,0:T(8,128)(2,1)} %param.13) | copy-start | bytes 1179652
  0.0 19.1 %copy-start.6 = (f32[256]{0:T(256)S(1)}, f32[256]{0:T(256)}, u32[]{:S(2)}) copy-start(f32[256]{0:T(256)} %param.20) | copy-start | bytes 3076
  0.0 19.1 %copy-start.5 = (f32[256]{0:T(256)S(1)}, f32[256]{0:T(256)}, u32[]{:S(2)}) copy-start(f32[256]{0:T(256)} %param.19) | copy-start | bytes 3076
  0.0 19.1 %copy-start.4 = (f32[256]{0:T(256)S(1)}, f32[256]{0:T(256)}, u32[]{:S(2)}) copy-start(f32[256]{0:T(256)} %param.16) | copy-start | bytes 3076
  0.0 19.1 %copy-start.2 = (bf16[7,7,256]{2,1,0:T(8,128)(2,1)S(1)}, bf16[7,7,256]{2,1,0:T(8,128)(2,1)}, u32[]{:S(2)}) copy-start(bf16[7,7,256]{2,1,0:T(8,128)(2,1)} %dw_kernel.1) | copy-start | bytes 75268
  0.0 19.1 %copy-start.3 = (bf16[48,256]{1,0:T(8,128)(2,1)S(1)}, bf16[48,256]{1,0:T(8,128)(2,1)}, u32[]{:S(2)}) copy-start(bf16[48,256]{1,0:T(8,128)(2,1)} %w_patch.1) | copy-start | bytes 73732
  0.9 9.2 %collective-permute-start.1 = (bf16[3,64,128]{2,1,0:T(8,128)(2,1)S(1)}, bf16[3,64,128]{2,1,0:T(8,128)(2,1)S(1)}, u32[]{:S(2)}, u32[]{:S(2)}) collective-permute-start(bf16[3,64,128]{2,1,0:T(8,128)(2,1)S(1)} %get-tuple-element.14), channel_id=1, source_target_pairs={{1,0},{2,1},{3,2},{4,3},{5,4},{6,5},{7,6},{8,7},{9,8},{10,9},{11,1... | collective-permute-start | bytes 147464 | tf_op jit(solution)/shard_map/ppermute | solution.py:23
  6.0 4.2 %collective-permute-start = (bf16[3,64,128]{2,1,0:T(8,128)(2,1)S(1)}, bf16[3,64,128]{2,1,0:T(8,128)(2,1)S(1)}, u32[]{:S(2)}, u32[]{:S(2)}) collective-permute-start(bf16[3,64,128]{2,1,0:T(8,128)(2,1)S(1)} %get-tuple-element.15), channel_id=1, source_target_pairs={{0,1},{1,2},{2,3},{3,4},{4,5},{5,6},{6,7},{7,8},{8,9},{9,10},{10,1... | collective-permute-start | bytes 147464 | tf_op jit(solution)/shard_map/ppermute | solution.py:23
  10.3 8.0 %collective-permute-start.2 = (bf16[3,16,1280]{2,1,0:T(8,128)(2,1)S(1)}, bf16[3,16,1280]{2,1,0:T(8,128)(2,1)S(1)}, u32[]{:S(2)}, u32[]{:S(2)}) collective-permute-start(bf16[3,16,1280]{2,1,0:T(8,128)(2,1)S(1)} %pad_maximum_fusion), channel_id=1, source_target_pairs={{0,32},{32,64},{64,96},{96,128},{128,160},{160,192},{192,224},{1,3... | collective-permute-start | bytes 368648 | tf_op jit(solution)/shard_map/ppermute | solution.py:23
  13.5 5.6 %collective-permute-start.3 = (bf16[3,16,1280]{2,1,0:T(8,128)(2,1)S(1)}, bf16[3,16,1280]{2,1,0:T(8,128)(2,1)S(1)}, u32[]{:S(2)}, u32[]{:S(2)}) collective-permute-start(bf16[3,16,1280]{2,1,0:T(8,128)(2,1)S(1)} %pad_maximum_fusion.1), channel_id=1, source_target_pairs={{32,0},{64,32},{96,64},{128,96},{160,128},{192,160},{224,192},{33,... | collective-permute-start | bytes 368648 | tf_op jit(solution)/shard_map/ppermute | solution.py:23
  19.1 1.0 copy-start

commit v4 on v3

--- a/solution.py
+++ b/solution.py
@@ -13,7 +13,7 @@
 ATTEND = 1024
 CONV_ROWS = 4
 CONV_BLOCKS = 1
-STEM = 11
+STEM = 22
 
 
 def exchange(last, first, axis):
@@ -42,17 +42,19 @@
 
 
 SPREAD = (
-    (1, 0, -5.25, 0, 5.25, 0, -1, 0),
-    (0, 1, 1, -4.25, -4.25, 1, 1, 0),
-    (0, -1, 1, 4.25, -4.25, -1, 1, 0),
-    (0, 0.5, 0.25, -2.5, -1.25, 2, 1, 0),
-    (0, -0.5, 0.25, 2.5, -1.25, -2, 1, 0),
-    (0, 2, 4, -2.5, -5, 0.5, 1, 0),
-    (0, -2, 4, 2.5, -5, -0.5, 1, 0),
-    (0, -1, 0, 5.25, 0, -5.25, 0, 1),
+    (9, 0, -48.25, 0, 52.5, 0, -14.25, 0, 1, 0),
+    (0, -9, -9, 39.25, 39.25, -13.25, -13.25, 1, 1, 0),
+    (0, 9, -9, -39.25, 39.25, 13.25, -13.25, -1, 1, 0),
+    (0, -4.5, -2.25, 23, 11.5, -20.5, -10.25, 2, 1, 0),
+    (0, 4.5, -2.25, -23, 11.5, 20.5, -10.25, -2, 1, 0),
+    (0, -18, -36, 24.5, 49, -7, -14, 0.5, 1, 0),
+    (0, 18, -36, -24.5, 49, 7, -14, -0.5, 1, 0),
+    (0, -3, -1, 15.75, 5.25, -15.75, -5.25, 3, 1, 0),
+    (0, 3, -1, -15.75, 5.25, 15.75, -5.25, -3, 1, 0),
+    (0, 9, 0, -48.25, 0, 52.5, 0, -14.25, 0, 1),
 )
-POINTS = (0, 1, -1, 2, -2, 0.5, -0.5)
-SCALE = (1, -2 / 9, -2 / 9, 1 / 90, 1 / 90, 32 / 45, 32 / 45, 1)
+NEAR = (0, 1, -1, 2, -2, 0.5, -0.5, 3, -3)
+SCALE = (1 / 9, 1 / 36, 1 / 36, -1 / 450, -1 / 450, -128 / 1575, -128 / 1575, 1 / 6300, 1 / 6300, 1)
 
 
 def stem(image, left, right, above, below, w_patch, dw_kernel, spread, taps, ordered, pixels, split):
@@ -102,25 +104,27 @@
     slot = place % 16
     pick = ones_where((slot < 12) & (source == slot * 4 + place // 16))
     weights = matmul(pick, w_patch[...]).astype(BF16)
-    offset = iota((64, 144), 1) - 5 - 2 * iota((64, 144), 0)
-    for point in range(8):
-        value = jnp.zeros((64, 144), F32)
-        for m in range(8):
+    offset = iota((32, 144), 1) - 5 - 4 * iota((32, 144), 0)
+    for point in range(10):
+        value = jnp.zeros((32, 144), F32)
+        for m in range(10):
             if SPREAD[point][m]:
                 value = jnp.where(offset == m, float(SPREAD[point][m]), value)
-        split[point * 64 : point * 64 + 64] = value.astype(BF16)
-    for parity in range(2):
-        split[512 + parity * 64 : 576 + parity * 64] = ones_where(offset == 3 + parity)
+        split[point * 32 : point * 32 + 32] = value.astype(BF16)
+    for place in range(4):
+        split[320 + place * 32 : 352 + place * 32] = ones_where(offset == 3 + place)
     place, source = iota((16, 7), 0), iota((16, 7), 1)
     powers = jnp.zeros((16, 7), F32)
-    for point in range(8):
+    for point in range(10):
         for j in range(7):
-            weight = float(POINTS[point] ** j) if point < 7 else float(j == 6)
+            weight = float(NEAR[point] ** j) if point < 9 else float(j == 6)
             if weight:
                 powers = jnp.where((place == point) & (source == j), weight, powers)
+    high = powers.astype(BF16)
+    low = (powers - high.astype(F32)).astype(BF16)
     for i in range(7):
-        value = matmul(powers.astype(BF16), dw_kernel[i])
-        for point in range(8):
+        value = matmul(high, dw_kernel[i]) + matmul(low, dw_kernel[i])
+        for point in range(10):
             taps[point, i] = jnp.broadcast_to(value[point : point + 1] * SCALE[point], taps.shape[2:])
 
     def step(row, carry):
@@ -137,7 +141,7 @@
 
 
 def conv_tile(spread, taps, mixed, row, rows, blocks):
-    chunks = 8 // blocks
+    chunks = 4 // blocks
 
     def step(index, carry):
         half = index // chunks
@@ -156,16 +160,23 @@
                             sums[r] = term if sums[r] is None else sums[r] + term
                 return sums
 
-            even, odd = products(0), products(7)
-            for point, factor in ((1, 1.0), (3, 2.0), (5, 0.5)):
+            first, last = products(0), products(9)
+            second, third = [0.0] * rows, [0.0] * rows
+            for point in (1, 3, 5, 7):
                 plus, minus = products(point), products(point + 1)
+                factor = float(NEAR[point])
                 for r in range(rows):
-                    even[r] = even[r] + (plus[r] + minus[r])
-                    gap = plus[r] - minus[r]
-                    odd[r] = odd[r] + (gap if factor == 1.0 else gap * factor)
-            for r in range(rows):
-                mixed[r, half, 0, block, :, lanes] = even[r]
-                mixed[r, half, 1, block, :, lanes] = odd[r]
+                    both, gap = plus[r] + minus[r], plus[r] - minus[r]
+                    first[r] = first[r] + both
+                    if point == 1:
+                        second[r], third[r], last[r] = gap, both, last[r] + gap
+                    else:
+                        second[r] = second[r] + gap * factor
+                        third[r] = third[r] + both * factor**2
+                        last[r] = last[r] + gap * factor**3
+            for place, found in enumerate((first, second, third, last)):
+                for r in range(rows):
+                    mixed[r, half, place, block, :, lanes] = found[r]
         return carry
 
     lax.fori_loop(0, 2 * chunks, step, 0)
@@ -208,7 +219,7 @@
             hidden = gelu_half(matmul(normed, w_up[:, start : start + 256])).astype(BF16)
             part = matmul(hidden, w_down[start : start + 256, :])
             down = part if down is None else down + part
-        center = spread[pl.ds(row + 3, per_tile), :, 8:10].reshape(TOKENS, width)
+        center = spread[pl.ds(row + 3, per_tile), :, 10:14].reshape(TOKENS, width)
         block = center + scale[...] * down
         features[pl.ds(pl.multiple_of(tile * TOKENS, TOKENS), TOKENS), :] = layer_norm(
             block, gain_two[...]
@@ -345,12 +356,12 @@
         in_specs=[pl.BlockSpec(memory_space=pltpu.VMEM)] * 11 + [pl.BlockSpec(memory_space=pl.ANY)] * 3,
         out_specs=pl.BlockSpec(memory_space=pltpu.VMEM),
         scratch_shapes=[
-            pltpu.VMEM((tile_rows + 6, 2, 10, 8, 8, width), F32),
-            pltpu.VMEM((8, 7, 8, width), F32),
+            pltpu.VMEM((tile_rows + 6, 2, 14, 4, 8, width), F32),
+            pltpu.VMEM((10, 7, 8, width), F32),
             pltpu.VMEM(((tile_rows + 6) * 16, breadth + 256), BF16),
             pltpu.VMEM((4, (tile_rows + 6) * 16, tile_cols + 128), BF16),
-            pltpu.VMEM((640, 144), BF16),
-            pltpu.VMEM((TOKENS // tile_cols, 2, 2, 8, 8, width), F32),
+            pltpu.VMEM((448, 144), BF16),
+            pltpu.VMEM((TOKENS // tile_cols, 2, 4, 4, 8, width), F32),
             pltpu.VMEM((tile_rows * tile_cols, width), BF16),
             pltpu.VMEM((width, HEADS * count), F32),
             pltpu.VMEM(w_up.shape, BF16),

time: 127 us -> 120 us (0.945)
  Pallas kernels: 51.5 us -> 44.5 us
    pallas_call x1, Pallas kernels: 45.1 us -> 38 us  [partial_sums(): pl.pallas_call(encoder, out_shape=jax.ShapeDtypeStruct((cols, HEADS * HEA...]
where the time goes in v4:
time: 120 us
  blocking collectives  57.9 us (48%)
  Pallas kernels  44.5 us (37%)
  starting transfers between devices  12.6 us (10%)
  local copies, waits for them, and re-layouts  3.04 us (3%)
    pallas_call x1, Pallas kernels, partial_sums(): pl.pallas_call(encoder, out_shape=jax.ShapeDtypeStruct((cols, HEADS * HEA...  38 us
    all_to_all x1, blocking collectives, body(): partial = merge_partials(lax.all_to_all(packed, 'cols', 0, 0))  29.4 us
    all_to_all x2, blocking collectives, share(): lax.all_to_all(jnp.broadcast_to(value, (size, *value.shape)), axis, 0, 0)  28.5 us
    ppermute x4, starting transfers between devices, exchange(): return (lax.ppermute(last, axis, up), lax.ppermute(first, axis, down))  12.6 us
    pallas_call x1, Pallas kernels, paired_queries(): pl.pallas_call(queries, out_shape=jax.ShapeDtypeStruct((HEADS // 2, 2 * H...  3.56 us
    pallas_call x1, Pallas kernels, body(): pl.pallas_call(project, out_shape=jax.ShapeDtypeStruct(latents.shape, F32...  2.93 us
  transfers between devices with their start and end apart: 4, of which 2 were waited for; matrix products, arithmetic and copies ran while one was open for 1% of the time, Pallas kernels for 3%

profile of v4, /device:TPU:1, one launch (start us, length us, event | category | flops | bytes accessed | tf_op | source)
XLA Modules:
  0.0 119.6 jit_solution(4768811988555569554)
XLA Ops:
  0.0 0.0 copy-start.1
  0.0 0.0 copy-start.6
  0.0 0.0 copy-start.5
  0.0 0.0 copy-start.4
  0.0 0.0 copy-start.2
  0.0 0.0 copy-start.3
  0.0 0.9 fusion.16
  0.9 5.1 %collective-permute-start.1 = (bf16[3,64,128]{2,1,0:T(8,128)(2,1)S(1)}, bf16[3,64,128]{2,1,0:T(8,128)(2,1)S(1)}, u32[]{:S(2)}, u32[]{:S(2)}) collective-permute-start(bf16[3,64,128]{2,1,0:T(8,128)(2,1)S(1)} %get-tuple-element.14), channel_id=1, source_target_pairs={{1,0},{2,1},{3,2},{4,3},{5,4},{6,5},{7,6},{8,7},{9,8},{10,9},{11,1... | collective-permute-start | bytes 147464 | tf_op jit(solution)/shard_map/ppermute | solution.py:23
  6.0 3.1 %collective-permute-start = (bf16[3,64,128]{2,1,0:T(8,128)(2,1)S(1)}, bf16[3,64,128]{2,1,0:T(8,128)(2,1)S(1)}, u32[]{:S(2)}, u32[]{:S(2)}) collective-permute-start(bf16[3,64,128]{2,1,0:T(8,128)(2,1)S(1)} %get-tuple-element.15), channel_id=1, source_target_pairs={{0,1},{1,2},{2,3},{3,4},{4,5},{5,6},{6,7},{7,8},{8,9},{9,10},{10,1... | collective-permute-start | bytes 147464 | tf_op jit(solution)/shard_map/ppermute | solution.py:23
  9.1 1.0 fusion.15
  10.1 0.0 collective-permute-done.1
  10.1 0.2 collective-permute-done
  10.3 3.1 %collective-permute-start.2 = (bf16[3,16,1280]{2,1,0:T(8,128)(2,1)S(1)}, bf16[3,16,1280]{2,1,0:T(8,128)(2,1)S(1)}, u32[]{:S(2)}, u32[]{:S(2)}) collective-permute-start(bf16[3,16,1280]{2,1,0:T(8,128)(2,1)S(1)} %pad_maximum_fusion), channel_id=1, source_target_pairs={{0,32},{32,64},{64,96},{96,128},{128,160},{160,192},{192,224},{1,3... | collective-permute-start | bytes 368648 | tf_op jit(solution)/shard_map/ppermute | solution.py:23
  13.5 1.3 %collective-permute-start.3 = (bf16[3,16,1280]{2,1,0:T(8,128)(2,1)S(1)}, bf16[3,16,1280]{2,1,0:T(8,128)(2,1)S(1)}, u32[]{:S(2)}, u32[]{:S(2)}) collective-permute-start(bf16[3,16,1280]{2,1,0:T(8,128)(2,1)S(1)} %pad_maximum_fusion.1), channel_id=1, source_target_pairs={{32,0},{64,32},{96,64},{128,96},{160,128},{192,160},{224,192},{33,... | collective-permute-start | bytes 368648 | tf_op jit(solution)/shard_map/ppermute | solution.py:23
  14.8 3.6 %queries.1.query = bf16[4,256,256]{2,1,0:T(8,128)(2,1)} custom-call(bf16[128,1024]{1,0:T(8,128)(2,1)} %latents.3, f32[1,1024]{1,0:T(1,128)} %bitcast.69, bf16[1024,1024]{1,0:T(8,128)(2,1)} %w_q.1), custom_call_target="tpu_custom_call" | custom-call | flops 268435456 | bytes 2097152 | tf_op jit(solution)/shard_map/queries/pallas_call | solution.py:334
  18.3 0.0 collective-permute-done.2
  18.3 0.8 collective-permute-done.3
  19.1 0.0 copy-done.1
  19.1 0.0 copy-done.6
  19.1 0.0 copy-done.5
  19.1 0.0 copy-done.4
  19.1 0.0 copy-done.2
  19.1 0.0 copy-done.3
  19.1 0.0 copy-start
  19.1 1.0 copy-done
  20.2 38.0 %encoder.1 = bf16[32,48,128]{2,1,0:T(8,128)(2,1)S(1)} custom-call(bf16[192,1024]{1,0:T(8,128)(2,1)S(1)} %bitcast.52, bf16[192,128]{1,0:T(8,128)(2,1)S(1)} %bitcast.56, bf16[192,128]{1,0:T(8,128)(2,1)S(1)} %bitcast.55, bf16[48,1280]{1,0:T(8,128)(2,1)S(1)} %bitcast.53, bf16[48,1280]{1,0:T(8,128)(2,1)S(1)} %bitcast.54, bf16[48,256]{1,0:T(8,128)(2,1)S(1)} %copy-done.3, ...), custom_call_target="tpu_custom_call" | custom-call | tf_op jit(solution)/shard_map/encoder/pallas_call | solution.py:353
  58.2 29.4 %all_to_all.15 = bf16[32,48,128]{2,1,0:T(8,128)(2,1)S(1)} all-to-all(bf16[32,48,128]{2,1,0:T(8,128)(2,1)S(1)} %encoder.1), channel_id=1, replica_groups=mesh['rows'=8,'cols'=32] {'cols'}, dimensions={0} | all-to-all | bytes 786432 | tf_op jit(solution)/shard_map/all_to_all | solution.py:425
  87.6 0.1 convert_element_type.12
  87.8 0.1 fusion
  88.0 10.5 %all_to_all.16 = bf16[8,48,128]{2,1,0:T(8,128)(2,1)S(1)} all-to-all(bf16[8,48,128]{2,1,0:T(8,128)(2,1)S(1)} %broadcast_in_dim.4), channel_id=1, replica_groups=mesh['rows'=8,'cols'=32] {'rows'}, dimensions={0} | all-to-all | bytes 196608 | tf_op jit(solution)/shard_map/all_to_all | solution.py:316
  98.7 18.0 %all_to_all.17 = bf16[32,32,128]{2,1,0:T(8,128)(2,1)} all-to-all(bf16[32,32,128]{2,1,0:T(8,128)(2,1)S(1)} %broadcast_in_dim.5), channel_id=1, replica_groups=mesh['rows'=8,'cols'=32] {'cols'}, dimensions={0} | all-to-all | bytes 524288 | tf_op jit(solution)/shard_map/all_to_all | solution.py:316
  116.6 2.9 %project.1 = f32[128,1024]{1,0:T(8,128)} custom-call(bf16[1024,128]{1,0:T(8,128)(2,1)} %bitcast.60, bf16[1024,1024]{1,0:T(8,128)(2,1)} %w_o.1, bf16[128,1024]{1,0:T(8,128)(2,1)} %latents.3), custom_call_target="tpu_custom_call" | custom-call | tf_op jit(solution)/shard_map/project/pallas_call | solution.py:428
  (22 shorter events, 0.4 us)
Async XLA Ops:
  0.0 19.1 %copy-start.1 = (bf16[3,64,1024]{2,1,0:T(8,128)(2,1)S(1)}, bf16[3,64,1024]{2,1,0:T(8,128)(2,1)}, u32[]{:S(2)}) copy-start(bf16[3,64,1024]{2,1,0:T(8,128)(2,1)} %param.13) | copy-start | bytes 1179652
  0.0 19.1 %copy-start.6 = (f32[256]{0:T(256)S(1)}, f32[256]{0:T(256)}, u32[]{:S(2)}) copy-start(f32[256]{0:T(256)} %param.20) | copy-start | bytes 3076
  0.0 19.1 %copy-start.5 = (f32[256]{0:T(256)S(1)}, f32[256]{0:T(256)}, u32[]{:S(2)}) copy-start(f32[256]{0:T(256)} %param.19) | copy-start | bytes 3076
  0.0 19.1 %copy-start.4 = (f32[256]{0:T(256)S(1)}, f32[256]{0:T(256)}, u32[]{:S(2)}) copy-start(f32[256]{0:T(256)} %param.16) | copy-start | bytes 3076
  0.0 19.1 %copy-start.2 = (bf16[7,7,256]{2,1,0:T(8,128)(2,1)S(1)}, bf16[7,7,256]{2,1,0:T(8,128)(2,1)}, u32[]{:S(2)}) copy-start(bf16[7,7,256]{2,1,0:T(8,128)(2,1)} %dw_kernel.1) | copy-start | bytes 75268
  0.0 19.1 %copy-start.3 = (bf16[48,256]{1,0:T(8,128)(2,1)S(1)}, bf16[48,256]{1,0:T(8,128)(2,1)}, u32[]{:S(2)}) copy-start(bf16[48,256]{1,0:T(8,128)(2,1)} %w_patch.1) | copy-start | bytes 73732
  0.9 9.2 %collective-permute-start.1 = (bf16[3,64,128]{2,1,0:T(8,128)(2,1)S(1)}, bf16[3,64,128]{2,1,0:T(8,128)(2,1)S(1)}, u32[]{:S(2)}, u32[]{:S(2)}) collective-permute-start(bf16[3,64,128]{2,1,0:T(8,128)(2,1)S(1)} %get-tuple-element.14), channel_id=1, source_target_pairs={{1,0},{2,1},{3,2},{4,3},{5,4},{6,5},{7,6},{8,7},{9,8},{10,9},{11,1... | collective-permute-start | bytes 147464 | tf_op jit(solution)/shard_map/ppermute | solution.py:23
  6.0 4.2 %collective-permute-start = (bf16[3,64,128]{2,1,0:T(8,128)(2,1)S(1)}, bf16[3,64,128]{2,1,0:T(8,128)(2,1)S(1)}, u32[]{:S(2)}, u32[]{:S(2)}) collective-permute-start(bf16[3,64,128]{2,1,0:T(8,128)(2,1)S(1)} %get-tuple-element.15), channel_id=1, source_target_pairs={{0,1},{1,2},{2,3},{3,4},{4,5},{5,6},{6,7},{7,8},{8,9},{9,10},{10,1... | collective-permute-start | bytes 147464 | tf_op jit(solution)/shard_map/ppermute | solution.py:23
  10.3 8.0 %collective-permute-start.2 = (bf16[3,16,1280]{2,1,0:T(8,128)(2,1)S(1)}, bf16[3,16,1280]{2,1,0:T(8,128)(2,1)S(1)}, u32[]{:S(2)}, u32[]{:S(2)}) collective-permute-start(bf16[3,16,1280]{2,1,0:T(8,128)(2,1)S(1)} %pad_maximum_fusion), channel_id=1, source_target_pairs={{0,32},{32,64},{64,96},{96,128},{128,160},{160,192},{192,224},{1,3... | collective-permute-start | bytes 368648 | tf_op jit(solution)/shard_map/ppermute | solution.py:23
  13.5 5.6 %collective-permute-start.3 = (bf16[3,16,1280]{2,1,0:T(8,128)(2,1)S(1)}, bf16[3,16,1280]{2,1,0:T(8,128)(2,1)S(1)}, u32[]{:S(2)}, u32[]{:S(2)}) collective-permute-start(bf16[3,16,1280]{2,1,0:T(8,128)(2,1)S(1)} %pad_maximum_fusion.1), channel_id=1, source_target_pairs={{32,0},{64,32},{96,64},{128,96},{160,128},{192,160},{224,192},{33,... | collective-permute-start | bytes 368648 | tf_op jit(solution)/shard_map/ppermute | solution.py:23
  19.1 1.0 copy-start

commit v5 on v4

--- a/solution.py
+++ b/solution.py
@@ -1,5 +1,6 @@
 import jax
 import jax.numpy as jnp
+import numpy as np
 from jax import lax
 from jax.experimental import pallas as pl
 from jax.experimental.pallas import tpu as pltpu
@@ -10,10 +11,9 @@
 F32 = jnp.float32
 BF16 = jnp.bfloat16
 TOKENS = 1024
-ATTEND = 1024
+ATTEND = 4096
 CONV_ROWS = 4
 CONV_BLOCKS = 1
-STEM = 22
 
 
 def exchange(last, first, axis):
@@ -57,45 +57,58 @@
 SCALE = (1 / 9, 1 / 36, 1 / 36, -1 / 450, -1 / 450, -128 / 1575, -128 / 1575, 1 / 6300, 1 / 6300, 1)
 
 
-def stem(image, left, right, above, below, w_patch, dw_kernel, spread, taps, ordered, pixels, split):
-    rows = spread.shape[0]
+def tile_parts(width, tiles):
+    result = []
+    for tile in range(tiles):
+        low = max(0, 512 * tile - 32) // 128 * 128
+        parts = [(low, min(width, 512 * tile + 512), low)]
+        if 512 * tile < 32:
+            parts.append((width, width + 128, -128))
+        if 512 * tile + 480 > width:
+            parts.append((width + 128, width + 256, width))
+        result.append(parts)
+    return result
+
+
+def tables(rows, width, tiles):
     local = (rows - 6) * 4
-    places = rows * 16
-
-    def pick_rows(count, first, wanted_of):
-        place, source = iota((places, count), 0), iota((places, count), 1)
-        slot = place % 16
-        pixel_row = (place // 16) * 4 + slot % 4 - first
-        return ones_where((slot < 12) & wanted_of(source, slot // 4, pixel_row))
-
-    pick = pick_rows(
-        3 * local, 12, lambda s, c, r: (r >= 0) & (r < local) & (s == c * local + r)
-    )
-    pick_above = pick_rows(48, -4, lambda s, c, r: (r < 16) & (s == c * 16 + r))
-    pick_below = pick_rows(48, 12 + local, lambda s, c, r: (r >= 0) & (s == c * 16 + r))
+    place = np.arange(rows * 16)[:, None]
+    slot = place % 16
+    pixel_row = place // 16 * 4 + slot % 4
+    result = []
+    spans = ((local, 12, 48, -48), (16, -4, 0, 48), (16, 12 + local, -48, None))
+    for height, first, begin, end in spans:
+        line = pixel_row - first
+        inside = (slot < 12) & (line >= 0) & (line < height)
+        table = inside & (np.arange(3 * height) == slot // 4 * height + line)
+        result.append(table[begin:end])
+    lane = np.arange(512)
+    for tile, parts in enumerate(tile_parts(width, tiles)):
+        wanted = 4 * (tile * 128 + lane % 128 - 8) + lane // 128
+        result += [np.arange(end - begin)[:, None] + first == wanted for begin, end, first in parts]
+    offset = np.arange(144) - 5 - 4 * np.arange(32)[:, None]
+    spread = [sum(value * (offset == m) for m, value in enumerate(line)) for line in SPREAD]
+    result.append(np.concatenate(spread + [1.0 * (offset == 3 + place) for place in range(4)]))
+    return [jnp.asarray(table.astype(np.float32), BF16) for table in result]
+
+
+def stem(image, left, right, above, below, w_patch, dw_kernel, chosen, taps, ordered, pixels):
+    pick, pick_above, pick_below, *splits = chosen
     width = image.shape[1]
+    below_row = ordered.shape[0] - 48
     for source, base in ((image, 0), (left, width), (right, width + 128)):
         step = min(256, source.shape[1])
         for start in range(0, source.shape[1], step):
             lanes = slice(base + start, base + start + step)
-            ordered[:, lanes] = (
-                matmul(pick, source[:, start : start + step])
-                + matmul(pick_above, above[:, lanes])
-                + matmul(pick_below, below[:, lanes])
+            ordered[48:below_row, lanes] = matmul(
+                pick[...], source[:, start : start + step]
             ).astype(BF16)
-    for tile in range(pixels.shape[2] // 128):
-        low = max(0, 512 * tile - 32) // 128 * 128
-        high = min(width, 512 * tile + 512)
-        parts = [(low, high, low)]
-        if 512 * tile < 32:
-            parts.append((width, width + 128, -128))
-        if 512 * tile + 480 > width:
-            parts.append((width + 128, width + 256, width))
+            ordered[:48, lanes] = matmul(pick_above[...], above[:, lanes]).astype(BF16)
+            ordered[below_row:, lanes] = matmul(pick_below[...], below[:, lanes]).astype(BF16)
+    for tile, parts in enumerate(tile_parts(width, pixels.shape[2] // 128)):
         found = None
-        for begin, end, first in parts:
-            lane, source = iota((end - begin, 512), 1), iota((end - begin, 512), 0)
-            wanted = 4 * (tile * 128 + lane % 128 - 8) + lane // 128
-            part = matmul(ordered[:, begin:end], ones_where(source + first == wanted))
+        for begin, end, _ in parts:
+            part = matmul(ordered[:, begin:end], splits.pop(0)[...])
             found = part if found is None else found + part
         found = found.astype(BF16)
         for phase in range(4):
@@ -104,15 +117,6 @@
     slot = place % 16
     pick = ones_where((slot < 12) & (source == slot * 4 + place // 16))
     weights = matmul(pick, w_patch[...]).astype(BF16)
-    offset = iota((32, 144), 1) - 5 - 4 * iota((32, 144), 0)
-    for point in range(10):
-        value = jnp.zeros((32, 144), F32)
-        for m in range(10):
-            if SPREAD[point][m]:
-                value = jnp.where(offset == m, float(SPREAD[point][m]), value)
-        split[point * 32 : point * 32 + 32] = value.astype(BF16)
-    for place in range(4):
-        split[320 + place * 32 : 352 + place * 32] = ones_where(offset == 3 + place)
     place, source = iota((16, 7), 0), iota((16, 7), 1)
     powers = jnp.zeros((16, 7), F32)
     for point in range(10):
@@ -127,17 +131,17 @@
         for point in range(10):
             taps[point, i] = jnp.broadcast_to(value[point : point + 1] * SCALE[point], taps.shape[2:])
 
-    def step(row, carry):
-        patches = jnp.concatenate(
-            [pixels[phase, pl.ds(pl.multiple_of(row * 16, 16), 16), :] for phase in range(4)], axis=0
-        )
-        value = matmul(patches, weights, ((0,), (0,))).astype(BF16)
-        for half in range(2):
-            found = matmul(split[...], value[half * 128 : half * 128 + 144])
-            spread[row, half] = found.reshape(spread.shape[2:])
-        return carry
-
-    lax.fori_loop(0, rows, step, 0, unroll=STEM)
+    return weights
+
+
+def stem_row(row, weights, split, spread, pixels):
+    patches = jnp.concatenate(
+        [pixels[phase, row * 16 : row * 16 + 16, :] for phase in range(4)], axis=0
+    )
+    value = matmul(patches, weights, ((0,), (0,))).astype(BF16)
+    for half in range(2):
+        found = matmul(split[...], value[half * 128 : half * 128 + 144])
+        spread[row, half] = found.reshape(spread.shape[2:])
 
 
 def conv_tile(spread, taps, mixed, row, rows, blocks):
@@ -189,44 +193,49 @@
 
 
 def encoder(
-    image, left, right, above, below, w_patch, dw_kernel, gain_one, scale, gain_two, query,
-    w_up_far, w_down_far, w_kv_far,
-    out, spread, taps, ordered, pixels, split, mixed, features, sums, w_up, w_down, w_kv, arrived,
+    image, left, right, above, below, w_patch, dw_kernel, gain_one, scale, gain_two,
+    w_up_far, w_down_far, w_kv_far, query_far, *rest,
 ):
+    *chosen, split = rest[:-13]
+    (
+        out, spread, taps, ordered, pixels, mixed, features, sums, w_up, w_down, w_kv, query, arrived,
+    ) = rest[-13:]
     width = spread.shape[5]
     tokens = features.shape[0]
     copies = [
         pltpu.make_async_copy(far, near, arrived.at[k])
-        for k, (far, near) in enumerate(((w_up_far, w_up), (w_down_far, w_down), (w_kv_far, w_kv)))
+        for k, (far, near) in enumerate(
+            ((w_up_far, w_up), (w_down_far, w_down), (w_kv_far, w_kv), (query_far, query))
+        )
     ]
     for copy in copies:
         copy.start()
-    stem(
-        image, left, right, above, below, w_patch, dw_kernel, spread, taps, ordered, pixels, split
+    weights = stem(
+        image, left, right, above, below, w_patch, dw_kernel, chosen, taps, ordered, pixels
     )
+    rows, per_tile = spread.shape[0], mixed.shape[0]
+    for row in range(per_tile + 6):
+        stem_row(row, weights, split, spread, pixels)
     for copy in copies:
         copy.wait()
     w_up[...] = w_up[...] * jnp.asarray(0.5, BF16)
-    per_tile = mixed.shape[0]
-    tiles = tokens // TOKENS
-
-    def block_step(tile, carry):
+    for tile in range(tokens // TOKENS):
         row = tile * per_tile
         conv_tile(spread, taps, mixed, row, CONV_ROWS, CONV_BLOCKS)
+        center = spread[row + 3 : row + 3 + per_tile, :, 10:14].reshape(TOKENS, width)
+        ahead = list(range(row + per_tile + 6, min(rows, row + 2 * per_tile + 6)))
         normed = layer_norm(mixed[...].reshape(TOKENS, width), gain_one[...]).astype(BF16)
         down = None
         for start in range(0, w_up.shape[1], 256):
             hidden = gelu_half(matmul(normed, w_up[:, start : start + 256])).astype(BF16)
             part = matmul(hidden, w_down[start : start + 256, :])
             down = part if down is None else down + part
-        center = spread[pl.ds(row + 3, per_tile), :, 10:14].reshape(TOKENS, width)
+            if ahead:
+                stem_row(ahead.pop(0), weights, split, spread, pixels)
         block = center + scale[...] * down
-        features[pl.ds(pl.multiple_of(tile * TOKENS, TOKENS), TOKENS), :] = layer_norm(
-            block, gain_two[...]
-        ).astype(BF16)
-        return carry
-
-    lax.fori_loop(0, tiles, block_step, 0)
+        features[tile * TOKENS : (tile + 1) * TOKENS, :] = layer_norm(block, gain_two[...]).astype(
+            BF16
+        )
     pair = 2 * HEAD_DIM
     sums[...] = jnp.zeros_like(sums)
     latents = out.shape[2]
@@ -350,24 +359,26 @@
     channels, height, breadth = image.shape
     tile_rows, tile_cols = height // 4, breadth // 4
     count, width = pairs.shape[2] // 2, w_patch.shape[1]
+    fixed = tables(tile_rows + 6, breadth, tile_cols // 128 + 1)
     return pl.pallas_call(
         encoder,
         out_shape=jax.ShapeDtypeStruct((cols, HEADS * HEAD_DIM // cols + 16, count), BF16),
-        in_specs=[pl.BlockSpec(memory_space=pltpu.VMEM)] * 11 + [pl.BlockSpec(memory_space=pl.ANY)] * 3,
+        in_specs=[pl.BlockSpec(memory_space=pltpu.VMEM)] * 10 + [pl.BlockSpec(memory_space=pl.ANY)] * 4
+        + [pl.BlockSpec(memory_space=pltpu.VMEM)] * len(fixed),
         out_specs=pl.BlockSpec(memory_space=pltpu.VMEM),
         scratch_shapes=[
             pltpu.VMEM((tile_rows + 6, 2, 14, 4, 8, width), F32),
             pltpu.VMEM((10, 7, 8, width), F32),
             pltpu.VMEM(((tile_rows + 6) * 16, breadth + 256), BF16),
             pltpu.VMEM((4, (tile_rows + 6) * 16, tile_cols + 128), BF16),
-            pltpu.VMEM((448, 144), BF16),
             pltpu.VMEM((TOKENS // tile_cols, 2, 4, 4, 8, width), F32),
             pltpu.VMEM((tile_rows * tile_cols, width), BF16),
             pltpu.VMEM((width, HEADS * count), F32),
             pltpu.VMEM(w_up.shape, BF16),
             pltpu.VMEM(w_down.shape, BF16),
             pltpu.VMEM(w_kv.shape, BF16),
-            pltpu.SemaphoreType.DMA((3,)),
+            pltpu.VMEM(pairs.shape, BF16),
+            pltpu.SemaphoreType.DMA((4,)),
         ],
         compiler_params=pltpu.CompilerParams(vmem_limit_bytes=52 * 2**20),
         name="encoder",
@@ -382,10 +393,11 @@
         gain_one.reshape(1, width),
         scale_block.reshape(1, width),
         gain_two.reshape(1, width),
-        pairs,
         w_up,
         w_down,
         w_kv,
+        pairs,
+        *fixed,
     )
 
 

time: 120 us -> 117 us (0.975)
  Pallas kernels: 44.5 us -> 42.6 us
    pallas_call x1, Pallas kernels: 38 us -> 36.1 us  [partial_sums(): pl.pallas_call(encoder, out_shape=jax.ShapeDtypeStruct((cols, HEADS * HEA...]
where the time goes in v5:
time: 117 us
  blocking collectives  57.9 us (49%)
  Pallas kernels  42.6 us (36%)
  starting transfers between devices  12.6 us (11%)
  local copies, waits for them, and re-layouts  2.17 us (2%)
    pallas_call x1, Pallas kernels, partial_sums(): pl.pallas_call(encoder, out_shape=jax.ShapeDtypeStruct((cols, HEADS * HEA...  36.1 us
    all_to_all x1, blocking collectives, body(): partial = merge_partials(lax.all_to_all(packed, 'cols', 0, 0))  29.4 us
    all_to_all x2, blocking collectives, share(): lax.all_to_all(jnp.broadcast_to(value, (size, *value.shape)), axis, 0, 0)  28.5 us
    ppermute x4, starting transfers between devices, exchange(): return (lax.ppermute(last, axis, up), lax.ppermute(first, axis, down))  12.6 us
    pallas_call x1, Pallas kernels, paired_queries(): pl.pallas_call(queries, out_shape=jax.ShapeDtypeStruct((HEADS // 2, 2 * H...  3.56 us
    pallas_call x1, Pallas kernels, body(): pl.pallas_call(project, out_shape=jax.ShapeDtypeStruct(latents.shape, F32...  2.92 us
  transfers between devices with their start and end apart: 4, of which 2 were waited for; matrix products, arithmetic and copies ran while one was open for 1% of the time, Pallas kernels for 3%

profile of v5, /device:TPU:1, one launch (start us, length us, event | category | flops | bytes accessed | tf_op | source)
XLA Modules:
  0.0 116.8 jit_solution(1486404024921116322)
XLA Ops:
  0.0 0.0 copy-start.2
  0.0 0.0 copy-start.3
  0.0 0.0 copy-start.1
  0.0 0.0 copy-start.7
  0.0 0.0 copy-start.8
  0.0 0.0 copy-start.4
  0.0 0.0 copy-start
  0.1 0.0 copy-start.11
  0.1 0.0 copy-start.10
  0.1 0.0 copy-start.9
  0.1 0.0 copy-start.5
  0.1 0.0 copy-start.6
  0.1 1.0 fusion.16
  1.1 5.1 %collective-permute-start.1 = (bf16[3,64,128]{2,1,0:T(8,128)(2,1)S(1)}, bf16[3,64,128]{2,1,0:T(8,128)(2,1)S(1)}, u32[]{:S(2)}, u32[]{:S(2)}) collective-permute-start(bf16[3,64,128]{2,1,0:T(8,128)(2,1)S(1)} %get-tuple-element.14), channel_id=1, source_target_pairs={{1,0},{2,1},{3,2},{4,3},{5,4},{6,5},{7,6},{8,7},{9,8},{10,9},{11,1... | collective-permute-start | bytes 147464 | tf_op jit(solution)/shard_map/ppermute | solution.py:23
  6.2 3.1 %collective-permute-start = (bf16[3,64,128]{2,1,0:T(8,128)(2,1)S(1)}, bf16[3,64,128]{2,1,0:T(8,128)(2,1)S(1)}, u32[]{:S(2)}, u32[]{:S(2)}) collective-permute-start(bf16[3,64,128]{2,1,0:T(8,128)(2,1)S(1)} %get-tuple-element.15), channel_id=1, source_target_pairs={{0,1},{1,2},{2,3},{3,4},{4,5},{5,6},{6,7},{7,8},{8,9},{9,10},{10,1... | collective-permute-start | bytes 147464 | tf_op jit(solution)/shard_map/ppermute | solution.py:23
  9.3 1.0 fusion.15
  10.3 0.0 collective-permute-done.1
  10.3 0.2 collective-permute-done
  10.5 3.1 %collective-permute-start.2 = (bf16[3,16,1280]{2,1,0:T(8,128)(2,1)S(1)}, bf16[3,16,1280]{2,1,0:T(8,128)(2,1)S(1)}, u32[]{:S(2)}, u32[]{:S(2)}) collective-permute-start(bf16[3,16,1280]{2,1,0:T(8,128)(2,1)S(1)} %pad_maximum_fusion), channel_id=1, source_target_pairs={{0,32},{32,64},{64,96},{96,128},{128,160},{160,192},{192,224},{1,3... | collective-permute-start | bytes 368648 | tf_op jit(solution)/shard_map/ppermute | solution.py:23
  13.7 1.3 %collective-permute-start.3 = (bf16[3,16,1280]{2,1,0:T(8,128)(2,1)S(1)}, bf16[3,16,1280]{2,1,0:T(8,128)(2,1)S(1)}, u32[]{:S(2)}, u32[]{:S(2)}) collective-permute-start(bf16[3,16,1280]{2,1,0:T(8,128)(2,1)S(1)} %pad_maximum_fusion.1), channel_id=1, source_target_pairs={{32,0},{64,32},{96,64},{128,96},{160,128},{192,160},{224,192},{33,... | collective-permute-start | bytes 368648 | tf_op jit(solution)/shard_map/ppermute | solution.py:23
  15.0 3.6 %queries.1.query_far = bf16[4,256,256]{2,1,0:T(8,128)(2,1)} custom-call(bf16[128,1024]{1,0:T(8,128)(2,1)} %latents.3, f32[1,1024]{1,0:T(1,128)} %bitcast.69, bf16[1024,1024]{1,0:T(8,128)(2,1)} %w_q.1), custom_call_target="tpu_custom_call" | custom-call | flops 268435456 | bytes 2097152 | tf_op jit(solution)/shard_map/queries/pallas_call | solution.py:343
  18.5 0.0 collective-permute-done.2
  18.5 0.8 collective-permute-done.3
  19.3 0.0 copy-done.2
  19.3 0.0 copy-done.3
  19.3 0.0 copy-done.1
  19.3 0.0 copy-done.7
  19.3 0.0 copy-done.8
  19.3 0.0 copy-done.4
  19.3 0.0 copy-done
  19.3 0.0 copy-done.11
  19.3 0.0 copy-done.10
  19.4 0.0 copy-done.9
  19.4 0.0 copy-done.5
  19.4 0.0 copy-done.6
  19.4 36.1 %encoder.1 = bf16[32,48,128]{2,1,0:T(8,128)(2,1)S(1)} custom-call(bf16[192,1024]{1,0:T(8,128)(2,1)S(1)} %bitcast.52, bf16[192,128]{1,0:T(8,128)(2,1)S(1)} %bitcast.56, bf16[192,128]{1,0:T(8,128)(2,1)S(1)} %bitcast.55, bf16[48,1280]{1,0:T(8,128)(2,1)S(1)} %bitcast.53, bf16[48,1280]{1,0:T(8,128)(2,1)S(1)} %bitcast.54, bf16[48,256]{1,0:T(8,128)(2,1)S(1)} %copy-done.6, ...), custom_call_target="tpu_custom_call" | custom-call | tf_op jit(solution)/shard_map/encoder/pallas_call | solution.py:363
  55.5 29.4 %all_to_all.15 = bf16[32,48,128]{2,1,0:T(8,128)(2,1)S(1)} all-to-all(bf16[32,48,128]{2,1,0:T(8,128)(2,1)S(1)} %encoder.1), channel_id=1, replica_groups=mesh['rows'=8,'cols'=32] {'cols'}, dimensions={0} | all-to-all | bytes 786432 | tf_op jit(solution)/shard_map/all_to_all | solution.py:437
  84.9 0.1 convert_element_type.12
  85.1 0.1 fusion
  85.3 10.5 %all_to_all.16 = bf16[8,48,128]{2,1,0:T(8,128)(2,1)S(1)} all-to-all(bf16[8,48,128]{2,1,0:T(8,128)(2,1)S(1)} %broadcast_in_dim.4), channel_id=1, replica_groups=mesh['rows'=8,'cols'=32] {'rows'}, dimensions={0} | all-to-all | bytes 196608 | tf_op jit(solution)/shard_map/all_to_all | solution.py:325
  96.0 17.9 %all_to_all.17 = bf16[32,32,128]{2,1,0:T(8,128)(2,1)} all-to-all(bf16[32,32,128]{2,1,0:T(8,128)(2,1)S(1)} %broadcast_in_dim.5), channel_id=1, replica_groups=mesh['rows'=8,'cols'=32] {'cols'}, dimensions={0} | all-to-all | bytes 524288 | tf_op jit(solution)/shard_map/all_to_all | solution.py:325
  113.9 2.9 %project.1 = f32[128,1024]{1,0:T(8,128)} custom-call(bf16[1024,128]{1,0:T(8,128)(2,1)} %bitcast.60, bf16[1024,1024]{1,0:T(8,128)(2,1)} %w_o.1, bf16[128,1024]{1,0:T(8,128)(2,1)} %latents.3), custom_call_target="tpu_custom_call" | custom-call | tf_op jit(solution)/shard_map/project/pallas_call | solution.py:440
  (22 shorter events, 0.4 us)
Async XLA Ops:
  0.0 19.3 %copy-start.2 = (bf16[448,144]{1,0:T(8,128)(2,1)S(1)}, bf16[448,144]{1,0:T(8,128)(2,1)}, u32[]{:S(2)}) copy-start(bf16[448,144]{1,0:T(8,128)(2,1)} %constant.31.clone.rest_8_) | copy-start | bytes 387076
  0.0 19.3 %copy-start.3 = (bf16[128,512]{1,0:T(8,128)(2,1)S(1)}, bf16[128,512]{1,0:T(8,128)(2,1)}, u32[]{:S(2)}) copy-start(bf16[128,512]{1,0:T(8,128)(2,1)} %constant.30.clone.rest_7_) | copy-start | bytes 393220
  0.0 19.3 %copy-start.1 = (bf16[128,512]{1,0:T(8,128)(2,1)S(1)}, bf16[128,512]{1,0:T(8,128)(2,1)}, u32[]{:S(2)}) copy-start(bf16[128,512]{1,0:T(8,128)(2,1)} %constant.28.clone.rest_4_.rest_6_) | copy-start | bytes 393220
  0.0 19.3 %copy-start.7 = (bf16[48,48]{1,0:T(8,128)(2,1)S(1)}, bf16[48,48]{1,0:T(8,128)(2,1)}, u32[]{:S(2)}) copy-start(bf16[48,48]{1,0:T(8,128)(2,1)} %constant.26.clone.rest_2_) | copy-start | bytes 13828
  0.0 19.3 %copy-start.8 = (bf16[48,48]{1,0:T(8,128)(2,1)S(1)}, bf16[48,48]{1,0:T(8,128)(2,1)}, u32[]{:S(2)}) copy-start(bf16[48,48]{1,0:T(8,128)(2,1)} %constant.25.clone.rest_1_) | copy-start | bytes 13828
  0.0 19.3 %copy-start.4 = (bf16[256,192]{1,0:T(8,128)(2,1)S(1)}, bf16[256,192]{1,0:T(8,128)(2,1)}, u32[]{:S(2)}) copy-start(bf16[256,192]{1,0:T(8,128)(2,1)} %constant.24.clone.rest_0_) | copy-start | bytes 294916
  0.0 19.3 %copy-start = (bf16[3,64,1024]{2,1,0:T(8,128)(2,1)S(1)}, bf16[3,64,1024]{2,1,0:T(8,128)(2,1)}, u32[]{:S(2)}) copy-start(bf16[3,64,1024]{2,1,0:T(8,128)(2,1)} %param.22) | copy-start | bytes 1179652
  0.1 19.3 %copy-start.11 = (f32[256]{0:T(256)S(1)}, f32[256]{0:T(256)}, u32[]{:S(2)}) copy-start(f32[256]{0:T(256)} %param.29) | copy-start | bytes 3076
  0.1 19.3 %copy-start.10 = (f32[256]{0:T(256)S(1)}, f32[256]{0:T(256)}, u32[]{:S(2)}) copy-start(f32[256]{0:T(256)} %param.28) | copy-start | bytes 3076
  0.1 19.3 %copy-start.9 = (f32[256]{0:T(256)S(1)}, f32[256]{0:T(256)}, u32[]{:S(2)}) copy-start(f32[256]{0:T(256)} %param.25) | copy-start | bytes 3076
  0.1 19.3 %copy-start.5 = (bf16[7,7,256]{2,1,0:T(8,128)(2,1)S(1)}, bf16[7,7,256]{2,1,0:T(8,128)(2,1)}, u32[]{:S(2)}) copy-start(bf16[7,7,256]{2,1,0:T(8,128)(2,1)} %dw_kernel.1) | copy-start | bytes 75268
  0.1 19.3 %copy-start.6 = (bf16[48,256]{1,0:T(8,128)(2,1)S(1)}, bf16[48,256]{1,0:T(8,128)(2,1)}, u32[]{:S(2)}) copy-start(bf16[48,256]{1,0:T(8,128)(2,1)} %w_patch.1) | copy-start | bytes 73732
  1.1 9.2 %collective-permute-start.1 = (bf16[3,64,128]{2,1,0:T(8,128)(2,1)S(1)}, bf16[3,64,128]{2,1,0:T(8,128)(2,1)S(1)}, u32[]{:S(2)}, u32[]{:S(2)}) collective-permute-start(bf16[3,64,128]{2,1,0:T(8,128)(2,1)S(1)} %get-tuple-element.14), channel_id=1, source_target_pairs={{1,0},{2,1},{3,2},{4,3},{5,4},{6,5},{7,6},{8,7},{9,8},{10,9},{11,1... | collective-permute-start | bytes 147464 | tf_op jit(solution)/shard_map/ppermute | solution.py:23
  6.2 4.3 %collective-permute-start = (bf16[3,64,128]{2,1,0:T(8,128)(2,1)S(1)}, bf16[3,64,128]{2,1,0:T(8,128)(2,1)S(1)}, u32[]{:S(2)}, u32[]{:S(2)}) collective-permute-start(bf16[3,64,128]{2,1,0:T(8,128)(2,1)S(1)} %get-tuple-element.15), channel_id=1, source_target_pairs={{0,1},{1,2},{2,3},{3,4},{4,5},{5,6},{6,7},{7,8},{8,9},{9,10},{10,1... | collective-permute-start | bytes 147464 | tf_op jit(solution)/shard_map/ppermute | solution.py:23
  10.5 8.0 %collective-permute-start.2 = (bf16[3,16,1280]{2,1,0:T(8,128)(2,1)S(1)}, bf16[3,16,1280]{2,1,0:T(8,128)(2,1)S(1)}, u32[]{:S(2)}, u32[]{:S(2)}) collective-permute-start(bf16[3,16,1280]{2,1,0:T(8,128)(2,1)S(1)} %pad_maximum_fusion), channel_id=1, source_target_pairs={{0,32},{32,64},{64,96},{96,128},{128,160},{160,192},{192,224},{1,3... | collective-permute-start | bytes 368648 | tf_op jit(solution)/shard_map/ppermute | solution.py:23
  13.7 5.6 %collective-permute-start.3 = (bf16[3,16,1280]{2,1,0:T(8,128)(2,1)S(1)}, bf16[3,16,1280]{2,1,0:T(8,128)(2,1)S(1)}, u32[]{:S(2)}, u32[]{:S(2)}) collective-permute-start(bf16[3,16,1280]{2,1,0:T(8,128)(2,1)S(1)} %pad_maximum_fusion.1), channel_id=1, source_target_pairs={{32,0},{64,32},{96,64},{128,96},{160,128},{192,160},{224,192},{33,... | collective-permute-start | bytes 368648 | tf_op jit(solution)/shard_map/ppermute | solution.py:23
